TPU v7x, 32 devices: a whole 2x2x4 slice. The times are simulated.
32 devices in a mesh: island: 8 (over y, x, core), local: 4 (over z).
Axes of the slice: x: 2, y: 2, z: 4, core: 2. Of those that a mesh axis runs over, the one named last changes fastest.
Arguments:
- acts: bfloat16 [4096, 1440], P(('island', 'local')), may hold values from -6 to 6
- grad_out: bfloat16 [4096, 1440], P(('island', 'local')), may hold values from -1.5 to 1.5
- expert_ids: int32 [4096, 4], P(('island', 'local')), may hold values from 0 to 31, all different within a row; in each aligned block of 128 rows (0 to 127, 128 to 255, ...) at most 24 rows name the same one
- route_probs: bfloat16 [4096, 4], P(('island', 'local')), may hold values from 0.049804688 to 0.69921875
- w_gate: bfloat16 [32, 1440, 1440], P(('island', 'local')), may hold values from -0.15625 to 0.15625
- w_up: bfloat16 [32, 1440, 1440], P(('island', 'local')), may hold values from -0.15625 to 0.15625
- w_down: bfloat16 [32, 1440, 1440], P(('island', 'local')), may hold values from -0.15625 to 0.15625
Outputs:
- grad_in: bfloat16 [4096, 1440], P(('island', 'local'))
- grad_probs: bfloat16 [4096, 4], P(('island', 'local'))
- grad_w_gate: bfloat16 [32, 1440, 1440], P(('island', 'local'))
- grad_w_up: bfloat16 [32, 1440, 1440], P(('island', 'local'))
- grad_w_down: bfloat16 [32, 1440, 1440], P(('island', 'local'))
Inputs may be any that keep to these rules, and one draw needn't show every extreme that they name: `expert_ids`: each row names 4 different experts. Among the 128 rows of one device no expert is named more than 24 times, and in some device some expert is named exactly 24 times.
All inputs are finite; a program needn't handle non-finite values.
Results may differ from a plain program's by a relative error of at most 0.0085.
Values may be sent and summed in bfloat16 or wider, within the bound.
No kernel may reach another device: no remote copies, remote signals or barrier semaphores. Data moves between devices by JAX's collectives and lax.ppermute only.
A program may use at most 128 MiB of HBM per device.

v0:
```python
import functools

import jax
import jax.numpy as jnp
from jax import lax
from jax.experimental import pallas as pl
from jax.experimental.pallas import tpu as pltpu
from jax.sharding import PartitionSpec as P

BF = jnp.bfloat16
F32 = jnp.float32


def up_to(n, m):
    return -(-n // m) * m


def dot(a, b, ca, cb):
    return lax.dot_general(a, b, (((ca,), (cb,)), ((), ())), preferred_element_type=F32)


def spread(block, n, me):
    def send(v, pairs):
        return lax.ppermute(v, "local", pairs)

    return [send(block, [(i, (i + s) % n) for i in range(n)]) for s in range(1, n)]


def home(part, s, n):
    return lax.ppermute(part, "local", [((i + s) % n, i) for i in range(n)])


def choose(ids, islands, n, local, cap):
    tokens = ids.shape[0]
    expert = jnp.arange(islands, dtype=F32) * n + local.astype(F32)
    named = jnp.sum((ids.T[None] == expert[:, None, None]).astype(F32), axis=1)
    before = jnp.triu(jnp.ones((tokens, tokens), BF), 1)
    rank = dot(named.astype(BF), before, 1, 0)
    slot = jnp.where(named > 0, rank, -1.0)
    hot = slot[:, None, :] == jnp.arange(cap, dtype=F32)[None, :, None]
    return hot.astype(BF).reshape(islands * cap, tokens)


def tiles(size, step):
    return [(i, min(step, size - i)) for i in range(0, size, step)]


VMEM = pl.BlockSpec(memory_space=pltpu.VMEM)
SMEM = pl.BlockSpec(memory_space=pltpu.SMEM)
HBM = pl.BlockSpec(memory_space=pl.ANY)
COST = pl.CostEstimate(flops=1 << 20, transcendentals=0, bytes_accessed=1 << 16)
LONG = pl.CostEstimate(flops=12_000_000_000, transcendentals=0, bytes_accessed=1 << 20)
GRANT = pltpu.CompilerParams(vmem_limit_bytes=56 << 20)


def slots_of(ids, experts, cap):
    topk, tokens = ids.shape
    named = jnp.zeros((experts.shape[0], tokens), F32)
    for k in range(topk):
        named += jnp.where(ids[k:k + 1, :] == experts, 1.0, 0.0)
    earlier = lax.broadcasted_iota(jnp.int32, (tokens, tokens), 0) < lax.broadcasted_iota(
        jnp.int32, (tokens, tokens), 1)
    rank = dot(named.astype(BF), jnp.where(earlier, 1.0, 0.0).astype(BF), 1, 0)
    slot = jnp.where(named > 0, rank, -1.0)
    place = lax.broadcasted_iota(jnp.int32, (experts.shape[0], cap, tokens), 1).astype(F32)
    hot = jnp.where(slot[:, None, :] == place, 1.0, 0.0)
    return hot.reshape(experts.shape[0] * cap, tokens)


def pick_kernel(width, meta, lane, islands, n, cap, topk, place_ref, *refs):
    blocks, (out_ref, hot_ref) = refs[:-2], refs[-2:]
    inner = place_ref[2] > 0

    def read(at, size):
        one = blocks[0][at:at + size, :]
        return one if len(blocks) == 1 else jnp.where(inner, one, blocks[1][at:at + size, :])

    label = read(width, meta)
    experts = lax.broadcasted_iota(jnp.int32, (islands, 1), 0) * n + place_ref[1]
    hot = slots_of(label[topk:2 * topk, :].astype(F32), experts.astype(F32), cap).astype(BF)
    hot_ref[...] = hot
    for rows, to in ((read(0, width), 0), (label, width), (read(width + meta, width), lane)):
        size = rows.shape[0]
        out_ref[:, :, to:to + size] = dot(hot, rows, 1, 1).reshape(islands, cap, size).astype(BF)


def pick(place, blocks, width, meta, lane, islands, n, cap, topk):
    return pl.pallas_call(
        functools.partial(pick_kernel, width, meta, lane, islands, n, cap, topk),
        out_shape=[jax.ShapeDtypeStruct((islands, cap, lane + width), BF),
                   jax.ShapeDtypeStruct((islands * cap, blocks[0].shape[1]), BF)],
        in_specs=[SMEM] + [VMEM] * len(blocks), out_specs=[VMEM] * 2,
        compiler_params=GRANT, cost_estimate=LONG, name="pick",
    )(place, *blocks)


def expert_kernel(width, hidden, lane, topk, n, step, place_ref, got_ref, wg_hbm, wu_hbm, wd_hbm, *refs):
    prev, ret_ref, ys_ref, a_ref, dh_ref, du_ref, wg, wu, wd, h_ref, u_ref, sems = (None,) * (12 - len(refs)) + refs
    loads = [pltpu.make_async_copy(src, dst, sems.at[i])
             for i, (src, dst) in enumerate(((wg_hbm, wg), (wu_hbm, wu), (wd_hbm, wd)))]
    for load in loads:
        load.start()

    probs = got_ref[:, width:width + topk].astype(F32)
    ids = got_ref[:, width + topk:width + 2 * topk].astype(F32)
    me = (place_ref[0] * n + place_ref[1]).astype(F32)
    mine = ids == me
    p = jnp.sum(jnp.where(mine, probs, 0.0), axis=1, keepdims=True)
    x = got_ref[:, :width]
    y = got_ref[:, lane:lane + width]
    ys_ref[...] = (p * y.astype(F32)).astype(BF)
    loads[0].wait()
    for at, size in tiles(hidden, step):
        h_ref[:, at:at + size] = dot(x, wg[:, at:at + size], 1, 0)
    loads[1].wait()
    for at, size in tiles(hidden, step):
        u_ref[:, at:at + size] = dot(x, wu[:, at:at + size], 1, 0)
    loads[2].wait()
    gp = jnp.zeros((x.shape[0], 1), F32)
    for at, size in tiles(hidden, step):
        cut = slice(at, at + size)
        g = dot(y, wd[cut, :], 1, 1)
        h, u = h_ref[:, cut], u_ref[:, cut]
        sig = jax.nn.sigmoid(h)
        act = h * sig
        a = (act * u).astype(BF)
        a_ref[:, cut] = a
        gp += jnp.sum(g * a.astype(F32), axis=1, keepdims=True)
        da = p * g
        dh_ref[:, cut] = (da * u * sig * (1.0 + h * (1.0 - sig))).astype(BF)
        du_ref[:, cut] = (da * act).astype(BF)
    dh, du = dh_ref[...], du_ref[...]
    islands, depth, cap, _ = ret_ref.shape
    if prev is not None:
        ret_ref[:, :depth - 1] = prev[...]
    for at, size in tiles(width, step):
        cut = slice(at, at + size)
        dx = dot(dh, wg[cut, :], 1, 1) + dot(du, wu[cut, :], 1, 1)
        ret_ref[:, depth - 1, :, cut] = dx.reshape(islands, cap, size).astype(BF)
    ret_ref[:, depth - 1, :, width:] = jnp.where(mine, gp, 0.0).reshape(islands, cap, topk).astype(BF)


def expert(place, got, wg, wu, wd, width, lane, topk, n, islands, prev=None):
    rows, hidden = got.shape[0], wg.shape[1]
    depth = 1 if prev is None else prev.shape[1] + 1
    cols = (width, hidden, hidden, hidden)
    before = [] if prev is None else [prev]
    outs = pl.pallas_call(
        functools.partial(expert_kernel, width, hidden, lane, topk, n, 384),
        out_shape=[jax.ShapeDtypeStruct((islands, depth, rows // islands, width + topk), BF)]
        + [jax.ShapeDtypeStruct((rows, c), BF) for c in cols],
        in_specs=[SMEM, VMEM] + [HBM] * 3 + [VMEM] * len(before),
        out_specs=[VMEM] * 5,
        scratch_shapes=[pltpu.VMEM(wg.shape, BF), pltpu.VMEM(wu.shape, BF), pltpu.VMEM(wd.shape, BF),
                        pltpu.VMEM((rows, hidden), F32), pltpu.VMEM((rows, hidden), F32),
                        pltpu.SemaphoreType.DMA((3,))],
        compiler_params=GRANT,
        cost_estimate=COST,
        name="expert",
    )(place, got, wg, wu, wd, *before)
    return outs[0], outs[1:]


def merge_kernel(topk, at, hot_ref, back_ref, *refs):
    islands, _, cap, cols = back_ref.shape
    rows = back_ref[:, at].astype(F32).reshape(islands * cap, cols).astype(BF)
    total = dot(hot_ref[...], rows, 0, 0)
    if len(refs) == 1:
        refs[0][...] = total.astype(BF)
        return
    for other in refs[:-2]:
        total += other[...].astype(F32)
    refs[-2][...] = total[:, :cols - topk].T.astype(BF)
    refs[-1][...] = total[:, cols - topk:].T.astype(BF)


def merge(hot, back, at, topk, others=()):
    cols, tokens = back.shape[3], hot.shape[1]
    outs = [(cols - topk, tokens), (topk, tokens)] if others else [(tokens, cols)]
    res = pl.pallas_call(
        functools.partial(merge_kernel, topk, at),
        out_shape=[jax.ShapeDtypeStruct(o, BF) for o in outs],
        in_specs=[VMEM] * (2 + len(others)), out_specs=[VMEM] * len(outs),
        compiler_params=GRANT, cost_estimate=COST, name="merge",
    )(hot, back, *others)
    return res if others else res[0]


def pack_kernel(acts_ref, probs_ref, ids_ref, grad_ref, out_ref):
    width, topk = acts_ref.shape[0], ids_ref.shape[0]
    meta = out_ref.shape[0] - 2 * width
    label = jnp.concatenate(
        [probs_ref[...].astype(F32), ids_ref[...].astype(F32),
         jnp.zeros((meta - 2 * topk, ids_ref.shape[1]), F32)], axis=0)
    out_ref[:width, :] = acts_ref[...]
    out_ref[width:width + meta, :] = label.astype(BF)
    out_ref[width + meta:, :] = grad_ref[...]


def pack(acts, probs, ids, grad, meta):
    width, tokens = acts.shape
    return pl.pallas_call(
        pack_kernel, out_shape=jax.ShapeDtypeStruct((2 * width + meta, tokens), BF),
        in_specs=[VMEM] * 4, out_specs=VMEM, compiler_params=GRANT, cost_estimate=COST, name="pack",
    )(acts, probs, ids, grad)


def weights_kernel(counts, *refs):
    stacks, at = [], 0
    for count in counts:
        stacks.append(jnp.concatenate([r[...] for r in refs[at:at + count]], axis=0))
        at += count
    for right, out in zip(stacks[1:], refs[at:]):
        out[0] = dot(stacks[0], right, 0, 0).astype(BF)


def weight_grads(left, rights, width, step=256):
    rows = sum(v.shape[0] for v in left)
    cols = [pl.BlockSpec((v.shape[0], step), lambda i: (0, i)) for v in left]
    full = [pl.BlockSpec(v.shape, lambda i: (0, 0)) for right in rights for v in right]
    outs = [right[0].shape[1] for right in rights]
    return pl.pallas_call(
        functools.partial(weights_kernel, [len(v) for v in (left, *rights)]), grid=(pl.cdiv(width, step),),
        out_shape=[jax.ShapeDtypeStruct((1, width, o), BF) for o in outs],
        in_specs=cols + full,
        out_specs=[pl.BlockSpec((1, step, o), lambda i: (0, i, 0)) for o in outs],
        compiler_params=GRANT, cost_estimate=LONG, name="weight_grads",
    )(*left, *[v for right in rights for v in right])


def line_of_four(acts, grad_out, expert_ids, route_probs, wg, wu, wd):
    islands, n = lax.axis_size("island"), lax.axis_size("local")
    island, local = lax.axis_index("island"), lax.axis_index("local")
    tokens, width = acts.shape
    topk = expert_ids.shape[1]
    cap = 3 * tokens * topk // (2 * islands * n)
    meta = up_to(2 * topk, 16)
    lane = up_to(width + meta, 128)
    inner = ((local == 1) | (local == 2)).astype(jnp.int32)
    place = jnp.stack([island, local, inner])
    outer, middle, ends = [(0, 1), (1, 0), (2, 3), (3, 2)], [(1, 2), (2, 1)], [(1, 0), (2, 3)]
    seal = lax.optimization_barrier

    def send(v, pairs):
        return lax.ppermute(v, "local", pairs)

    def a2a(v):
        return lax.all_to_all(v, "island", 0, 0, tiled=True)

    def take(*blocks):
        return pick(place, blocks, width, meta, lane, islands, n, cap, topk)

    def deal(rows):
        return a2a(rows).reshape(islands * cap, -1)

    def work(got, prev=None):
        return expert(place, got, wg, wu, wd, width, lane, topk, n, islands, prev)

    def part(total, s):
        return send(total, [(i, i ^ s) for i in range(n)])

    own = pack(acts.T, route_probs.T, expert_ids.T, grad_out.T, meta)
    rows0, hot0 = take(own)
    got0 = deal(rows0)
    one, near, rows0 = seal((send(own, outer), send(own, middle), rows0))
    two_in, two_out = send(one, middle), send(near, ends)
    rows1, hot1 = take(one)
    got0, rows1 = seal((got0, rows1))
    got1 = deal(rows1)
    ret0, keep0 = work(got0)
    two_in, two_out, ret0 = seal((two_in, two_out, ret0))
    three = send(two_in, ends)
    rows2, hot2 = take(two_in, two_out)
    got1, rows2, keep0 = seal((got1, rows2, keep0))
    got2 = deal(rows2)
    ret1, keep1 = work(got1)
    three, ret1 = seal((three, ret1))
    rows3, hot3 = take(near, three)
    got2, rows3, keep1 = seal((got2, rows3, keep1))
    got3 = deal(rows3)
    ret12, keep2 = work(got2, ret1)
    got3, ret12, keep2 = seal((got3, ret12, keep2))
    back12 = a2a(ret12)
    ret3, keep3 = work(got3)
    merge1, merge2 = merge(hot1, back12, 0, topk), merge(hot2, back12, 1, topk)
    part1, part2 = part(merge1, 1), part(merge2, 2)
    merge1, merge2, ret3, keep3 = seal((merge1, merge2, ret3, keep3))
    back3 = a2a(ret3)
    ys, a, dh, du = zip(keep0, keep1, keep2, keep3)
    gg, gu = weight_grads((got0, got1, got2, got3), (dh, du), width)
    back3, gg, ret0 = seal((back3, gg, ret0))
    merge3 = merge(hot3, back3, 0, topk)
    part3 = part(merge3, 3)
    part1, part2, merge3, ret0, a = seal((part1, part2, merge3, ret0, a))
    back0 = a2a(ret0)
    gd, = weight_grads(a, (ys,), wd.shape[0])
    grad_in, grad_probs = merge(hot0, back0, 0, topk, (part1, part2, part3))
    return grad_in.T, grad_probs.T, gg, gu, gd


def shards(acts, grad_out, expert_ids, route_probs, w_gate, w_up, w_down):
    islands, n = lax.axis_size("island"), lax.axis_size("local")
    local = lax.axis_index("local")
    me = lax.axis_index("island") * n + local
    tokens, width = acts.shape
    topk = expert_ids.shape[1]
    cap = 3 * tokens * topk // (2 * islands * n)
    lane = up_to(width + 2 * topk, 128)
    wg, wu, wd = w_gate[0], w_up[0], w_down[0]
    if n == 4 and islands & (islands - 1) == 0 and cap % 8 == 0:
        return line_of_four(acts, grad_out, expert_ids, route_probs, wg, wu, wd)

    own = jnp.concatenate(
        [acts, route_probs, expert_ids.astype(BF),
         jnp.zeros((tokens, lane - width - 2 * topk), BF), grad_out], axis=1)

    def a2a(v):
        return lax.all_to_all(v, "island", 0, 0, tiled=True)

    def plain_pick(block):
        hot = choose(block[:, width + topk:width + 2 * topk].astype(F32), islands, n, local, cap)
        return hot, dot(hot, block, 1, 0).astype(BF).reshape(islands, cap, -1)

    def plain_expert(got):
        got = got.reshape(islands * cap, -1)
        x, y = got[:, :width], got[:, lane:]
        probs = got[:, width:width + topk].astype(F32)
        mine = got[:, width + topk:width + 2 * topk].astype(F32) == me.astype(F32)
        p = jnp.sum(jnp.where(mine, probs, 0.0), axis=1, keepdims=True)
        h, u, g = dot(x, wg, 1, 0), dot(x, wu, 1, 0), dot(y, wd, 1, 1)
        sig = jax.nn.sigmoid(h)
        act = h * sig
        a = (act * u).astype(BF)
        gp = jnp.sum(g * a.astype(F32), axis=1, keepdims=True)
        ys = (p * y.astype(F32)).astype(BF)
        da = p * g
        dh = (da * u * sig * (1.0 + h * (1.0 - sig))).astype(BF)
        du = (da * act).astype(BF)
        dx = (dot(dh, wg, 1, 1) + dot(du, wu, 1, 1)).astype(BF)
        ret = jnp.concatenate([dx, jnp.where(mine, gp, 0.0).astype(BF)], axis=1)
        return (x, ys, a, dh, du), ret.reshape(islands, cap, -1)

    def plain_merge(hot, back):
        return dot(hot, back.reshape(islands * cap, -1), 0, 0)

    kept, parts = [], []
    for s, block in enumerate([own] + spread(own, n, local)):
        hot, rows = plain_pick(block)
        k, ret = plain_expert(a2a(rows))
        kept.append(k)
        part = plain_merge(hot, a2a(ret))
        parts.append(part if s == 0 else home(part.astype(BF), s, n).astype(F32))
    x, ys, a, dh, du = (jnp.concatenate(v, axis=0) for v in zip(*kept))
    total = sum(parts[1:], parts[0])
    gg, gu, gd = (dot(l, r, 0, 0).astype(BF)[None] for l, r in ((x, dh), (x, du), (a, ys)))
    return (
        total[:, :width].astype(BF),
        total[:, width:].astype(BF),
        gg,
        gu,
        gd,
    )


def solution(mesh):
    rows = P(("island", "local"), None)
    mats = P(("island", "local"), None, None)
    return jax.shard_map(shards, mesh=mesh, in_specs=(rows,) * 4 + (mats,) * 3,
                         out_specs=(rows,) * 2 + (mats,) * 3, check_vma=False)
```

profile of v0, /device:TPU:10, one launch (start us, length us, event | category | flops | bytes accessed | tf_op | source)
XLA Modules:
  0.0 169.2 jit_solution(4686062189943053852)
XLA Ops:
  0.6 2.0 %pack.1.refs_0_ = bf16[2896,128]{1,0:T(8,128)(2,1)} custom-call(bf16[1440,128]{1,0:T(8,128)(2,1)} %bitcast.36, bf16[4,128]{1,0:T(4,128)(2,1)} %bitcast.39, s32[4,128]{1,0:T(4,128)} %bitcast.38, bf16[1440,128]{1,0:T(8,128)(2,1)} %bitcast.37), custom_call_target="tpu_custom_call" | custom-call | flops 1048576 | bytes 65536 | tf_op jit(solution)/shard_map/pack/pallas_call | solution.py:202
  2.7 3.5 %collective-permute-start.1 = (bf16[2896,128]{1,0:T(8,128)(2,1)}, bf16[2896,128]{1,0:T(8,128)(2,1)S(1)}, u32[]{:S(2)}, u32[]{:S(2)}) collective-permute-start(bf16[2896,128]{1,0:T(8,128)(2,1)} %pack.1.refs_0_), channel_id=1, source_target_pairs={{1,2},{2,1},{5,6},{6,5},{9,10},{10,9},{13,14},{14,13},{17,18},{18,... | collective-permute-start | bytes 2224136 | tf_op jit(solution)/shard_map/ppermute | solution.py:245
  6.2 0.1 collective-permute-start
  6.2 0.7 pad_add_fusion.place_ref
  6.9 2.7 %pick.4 = (bf16[8,24,2976]{2,1,0:T(8,128)(2,1)}, bf16[192,128]{1,0:T(8,128)(2,1)}) custom-call(s32[3]{0:T(128)} %pad_add_fusion.place_ref, bf16[2896,128]{1,0:T(8,128)(2,1)} %pack.1.refs_0_), custom_call_target="tpu_custom_call" | custom-call | flops 12000000000 | bytes 1048576 | tf_op jit(solution)/shard_map/pick/pallas_call | solution.py:88
  9.6 4.3 %all-to-all-start = ((bf16[8,24,2976]{2,1,0:T(8,128)(2,1)}), bf16[8,24,2976]{2,1,0:T(8,128)(2,1)S(1)}, u32[]{:S(2)}, u32[]{:S(2)}) async-start(bf16[8,24,2976]{2,1,0:T(8,128)(2,1)} %get-tuple-element.80), calls=%async_computation | async-start | bytes 2359296 | tf_op jit(solution)/shard_map/all_to_all | solution.py:248
  13.9 9.2 %collective-permute-done.1.refs_0_ = bf16[2896,128]{1,0:T(8,128)(2,1)S(1)} collective-permute-done((bf16[2896,128]{1,0:T(8,128)(2,1)}, bf16[2896,128]{1,0:T(8,128)(2,1)S(1)}, u32[]{:S(2)}, u32[]{:S(2)}) %collective-permute-start.1) | collective-permute-done | bytes 741408 | tf_op jit(solution)/shard_map/ppermute | solution.py:245
  23.1 1.5 collective-permute-done.refs_0_
  24.6 2.3 %collective-permute-start.2 = (bf16[2896,128]{1,0:T(8,128)(2,1)}, bf16[2896,128]{1,0:T(8,128)(2,1)}, u32[]{:S(2)}, u32[]{:S(2)}) collective-permute-start(bf16[2896,128]{1,0:T(8,128)(2,1)} %collective-permute-done.refs_0_), channel_id=1, source_target_pairs={{1,2},{2,1},{5,6},{6,5},{9,10},{10,9},{13,14},{14,13},{17,18},{18,... | collective-permute-start | bytes 2224136 | tf_op jit(solution)/shard_map/ppermute | solution.py:245
  26.9 2.3 %collective-permute-start.3 = (bf16[2896,128]{1,0:T(8,128)(2,1)S(1)}, bf16[2896,128]{1,0:T(8,128)(2,1)}, u32[]{:S(2)}, u32[]{:S(2)}) collective-permute-start(bf16[2896,128]{1,0:T(8,128)(2,1)S(1)} %collective-permute-done.1.refs_0_), channel_id=1, source_target_pairs={{1,0},{2,3},{5,4},{6,7},{9,8},{10,11},{13,12},{14,15},{17,16},{18,... | collective-permute-start | bytes 2224136 | tf_op jit(solution)/shard_map/ppermute | solution.py:245
  29.2 2.7 %pick.5 = (bf16[8,24,2976]{2,1,0:T(8,128)(2,1)}, bf16[192,128]{1,0:T(8,128)(2,1)}) custom-call(s32[3]{0:T(128)} %pad_add_fusion.place_ref, bf16[2896,128]{1,0:T(8,128)(2,1)} %collective-permute-done.refs_0_), custom_call_target="tpu_custom_call" | custom-call | flops 12000000000 | bytes 1048576 | tf_op jit(solution)/shard_map/pick/pallas_call | solution.py:88
  31.9 0.0 copy-start.2
  31.9 1.0 copy-done.2
  33.0 4.3 %all-to-all-start.1 = ((bf16[8,24,2976]{2,1,0:T(8,128)(2,1)}), bf16[8,24,2976]{2,1,0:T(8,128)(2,1)S(1)}, u32[]{:S(2)}, u32[]{:S(2)}) async-start(bf16[8,24,2976]{2,1,0:T(8,128)(2,1)} %get-tuple-element.84), calls=%async_computation.1 | async-start | bytes 2359296 | tf_op jit(solution)/shard_map/all_to_all | solution.py:248
  37.2 12.0 %expert.4 = (bf16[8,1,24,1444]{3,2,1,0:T(8,128)(2,1)}, bf16[192,1440]{1,0:T(8,128)(2,1)}, bf16[192,1440]{1,0:T(8,128)(2,1)}, bf16[192,1440]{1,0:T(8,128)(2,1)}, bf16[192,1440]{1,0:T(8,128)(2,1)}) custom-call(s32[3]{0:T(128)} %pad_add_fusion.place_ref, bf16[192,2976]{1,0:T(8,128)(2,1)} %bitcast.30, bf16[1440,1440]{1,0:T(8,128)(2,1)} %bitcast.16, ...), custom_call_target="tpu_custom_call" | custom-call | flops 1048576 | bytes 65536 | tf_op jit(solution)/shard_map/expert/pallas_call | solution.py:148
  49.2 2.0 %collective-permute-start.4 = (bf16[2896,128]{1,0:T(8,128)(2,1)}, bf16[2896,128]{1,0:T(8,128)(2,1)S(1)}, u32[]{:S(2)}, u32[]{:S(2)}) collective-permute-start(bf16[2896,128]{1,0:T(8,128)(2,1)} %collective-permute-done.2.refs_0_), channel_id=1, source_target_pairs={{1,0},{2,3},{5,4},{6,7},{9,8},{10,11},{13,12},{14,15},{17,16},{18,... | collective-permute-start | bytes 2224136 | tf_op jit(solution)/shard_map/ppermute | solution.py:245
  51.2 3.0 %pick.6 = (bf16[8,24,2976]{2,1,0:T(8,128)(2,1)}, bf16[192,128]{1,0:T(8,128)(2,1)}) custom-call(s32[3]{0:T(128)} %pad_add_fusion.place_ref, bf16[2896,128]{1,0:T(8,128)(2,1)} %collective-permute-done.2.refs_0_, bf16[2896,128]{1,0:T(8,128)(2,1)} %collective-permute-done.3.refs_1_), custom_call_target="tpu_custom_call" | custom-call | flops 12000000000 | bytes 1048576 | tf_op jit(solution)/shard_map/pick/pallas_call | solution.py:88
  54.2 1.0 copy-done.3
  55.2 4.2 %all-to-all-start.2 = ((bf16[8,24,2976]{2,1,0:T(8,128)(2,1)}), bf16[8,24,2976]{2,1,0:T(8,128)(2,1)S(1)}, u32[]{:S(2)}, u32[]{:S(2)}) async-start(bf16[8,24,2976]{2,1,0:T(8,128)(2,1)} %get-tuple-element.95), calls=%async_computation.2 | async-start | bytes 2359296 | tf_op jit(solution)/shard_map/all_to_all | solution.py:248
  59.4 12.0 %expert.5 = (bf16[8,1,24,1444]{3,2,1,0:T(8,128)(2,1)}, bf16[192,1440]{1,0:T(8,128)(2,1)}, bf16[192,1440]{1,0:T(8,128)(2,1)}, bf16[192,1440]{1,0:T(8,128)(2,1)}, bf16[192,1440]{1,0:T(8,128)(2,1)}) custom-call(s32[3]{0:T(128)} %pad_add_fusion.place_ref, bf16[192,2976]{1,0:T(8,128)(2,1)} %bitcast.32, bf16[1440,1440]{1,0:T(8,128)(2,1)} %bitcast.17, ...), custom_call_target="tpu_custom_call" | custom-call | flops 1048576 | bytes 65536 | tf_op jit(solution)/shard_map/expert/pallas_call | solution.py:148
  71.4 0.0 collective-permute-done.4.refs_1_
  71.4 0.0 copy-start.11
  71.4 0.9 copy-done.11
  72.3 3.0 %pick.7 = (bf16[8,24,2976]{2,1,0:T(8,128)(2,1)}, bf16[192,128]{1,0:T(8,128)(2,1)}) custom-call(s32[3]{0:T(128)} %pad_add_fusion.place_ref, bf16[2896,128]{1,0:T(8,128)(2,1)} %copy-done.10, bf16[2896,128]{1,0:T(8,128)(2,1)} %copy-done.11), custom_call_target="tpu_custom_call" | custom-call | flops 12000000000 | bytes 1048576 | tf_op jit(solution)/shard_map/pick/pallas_call | solution.py:88
  75.3 1.0 copy-done.1
  76.3 4.4 %all-to-all-start.3 = ((bf16[8,24,2976]{2,1,0:T(8,128)(2,1)}), bf16[8,24,2976]{2,1,0:T(8,128)(2,1)S(1)}, u32[]{:S(2)}, u32[]{:S(2)}) async-start(bf16[8,24,2976]{2,1,0:T(8,128)(2,1)} %get-tuple-element.104), calls=%async_computation.3 | async-start | bytes 2359296 | tf_op jit(solution)/shard_map/all_to_all | solution.py:248
  80.7 12.3 %expert.6 = (bf16[8,2,24,1444]{3,2,1,0:T(8,128)(2,1)}, bf16[192,1440]{1,0:T(8,128)(2,1)}, bf16[192,1440]{1,0:T(8,128)(2,1)}, bf16[192,1440]{1,0:T(8,128)(2,1)}, bf16[192,1440]{1,0:T(8,128)(2,1)}) custom-call(s32[3]{0:T(128)} %pad_add_fusion.place_ref, bf16[192,2976]{1,0:T(8,128)(2,1)} %bitcast.28, bf16[1440,1440]{1,0:T(8,128)(2,1)} %bitcast.18, ...), custom_call_target="tpu_custom_call" | custom-call | flops 1048576 | bytes 65536 | tf_op jit(solution)/shard_map/expert/pallas_call | solution.py:148
  93.1 3.0 %all-to-all-done.3 = bf16[8,24,2976]{2,1,0:T(8,128)(2,1)S(1)} async-done(((bf16[8,24,2976]{2,1,0:T(8,128)(2,1)}), bf16[8,24,2976]{2,1,0:T(8,128)(2,1)S(1)}, u32[]{:S(2)}, u32[]{:S(2)}) %all-to-all-start.3) | async-done | bytes 1142816 | tf_op jit(solution)/shard_map/all_to_all | solution.py:248
  96.1 1.0 copy-done.4
  97.1 5.0 %all-to-all-start.4 = ((bf16[8,2,24,1444]{3,2,1,0:T(8,128)(2,1)}), bf16[8,2,24,1444]{3,2,1,0:T(8,128)(2,1)S(1)}, u32[]{:S(2)}, u32[]{:S(2)}) async-start(bf16[8,2,24,1444]{3,2,1,0:T(8,128)(2,1)} %get-tuple-element.112), calls=%async_computation.4 | async-start | bytes 2359296 | tf_op jit(solution)/shard_map/all_to_all | solution.py:248
  102.1 12.0 %expert.7 = (bf16[8,1,24,1444]{3,2,1,0:T(8,128)(2,1)}, bf16[192,1440]{1,0:T(8,128)(2,1)}, bf16[192,1440]{1,0:T(8,128)(2,1)}, bf16[192,1440]{1,0:T(8,128)(2,1)}, bf16[192,1440]{1,0:T(8,128)(2,1)}) custom-call(s32[3]{0:T(128)} %pad_add_fusion.place_ref, bf16[192,2976]{1,0:T(8,128)(2,1)} %bitcast.34, bf16[1440,1440]{1,0:T(8,128)(2,1)} %bitcast.19, ...), custom_call_target="tpu_custom_call" | custom-call | flops 1048576 | bytes 65536 | tf_op jit(solution)/shard_map/expert/pallas_call | solution.py:148
  114.1 3.3 %all-to-all-done.4.back_ref = bf16[8,2,24,1444]{3,2,1,0:T(8,128)(2,1)S(1)} async-done(((bf16[8,2,24,1444]{3,2,1,0:T(8,128)(2,1)}), bf16[8,2,24,1444]{3,2,1,0:T(8,128)(2,1)S(1)}, u32[]{:S(2)}, u32[]{:S(2)}) %all-to-all-start.4) | async-done | bytes 1109024 | tf_op jit(solution)/shard_map/all_to_all | solution.py:248
  117.4 1.0 copy-done
  118.4 2.3 %merge.4 = bf16[128,1444]{1,0:T(8,128)(2,1)} custom-call(bf16[192,128]{1,0:T(8,128)(2,1)} %get-tuple-element.82.hot_ref, bf16[8,2,24,1444]{3,2,1,0:T(8,128)(2,1)} %copy-done), custom_call_target="tpu_custom_call" | custom-call | flops 1048576 | bytes 65536 | tf_op jit(solution)/shard_map/merge/pallas_call | solution.py:180
  120.8 2.4 %merge.5 = bf16[128,1444]{1,0:T(8,128)(2,1)} custom-call(bf16[192,128]{1,0:T(8,128)(2,1)} %get-tuple-element.113.hot_ref, bf16[8,2,24,1444]{3,2,1,0:T(8,128)(2,1)} %copy-done), custom_call_target="tpu_custom_call" | custom-call | flops 1048576 | bytes 65536 | tf_op jit(solution)/shard_map/merge/pallas_call | solution.py:180
  123.1 2.3 %collective-permute-start.6 = (bf16[128,1444]{1,0:T(8,128)(2,1)}, bf16[128,1444]{1,0:T(8,128)(2,1)S(1)}, u32[]{:S(2)}, u32[]{:S(2)}) collective-permute-start(bf16[128,1444]{1,0:T(8,128)(2,1)} %merge.5), channel_id=1, source_target_pairs={{0,2},{1,3},{2,0},{3,1},{4,6},{5,7},{6,4},{7,5},{8,10},{9,11},{10,... | collective-permute-start | bytes 1109000 | tf_op jit(solution)/shard_map/ppermute | solution.py:245
  125.4 5.0 %all-to-all-start.5 = ((bf16[8,1,24,1444]{3,2,1,0:T(8,128)(2,1)}), bf16[8,1,24,1444]{3,2,1,0:T(8,128)(2,1)S(1)}, u32[]{:S(2)}, u32[]{:S(2)}) async-start(bf16[8,1,24,1444]{3,2,1,0:T(8,128)(2,1)} %get-tuple-element.121), calls=%async_computation.5 | async-start | bytes 1179648 | tf_op jit(solution)/shard_map/all_to_all | solution.py:248
  130.4 12.4 %weight_grads.2 = (bf16[1,1440,1440]{2,1,0:T(8,128)(2,1)}, bf16[1,1440,1440]{2,1,0:T(8,128)(2,1)}) custom-call(bf16[192,2976]{1,0:T(8,128)(2,1)} %bitcast.31, bf16[192,2976]{1,0:T(8,128)(2,1)} %bitcast.33, bf16[192,2976]{1,0:T(8,128)(2,1)} %bitcast.29, bf16[192,2976]{1,0:T(8,128)(2,1)} %bitcast.35, bf16[192,1440]{1,0:T(8,128)(2,1)} %get-tuple-element.122.refs_4_, ...), custom_call_target="tpu_custom_call" | custom-call | flops 12000000000 | bytes 1048576 | tf_op jit(solution)/shard_map/weight_grads/pallas_call | solution.py:222
  142.8 0.0 copy-start.6
  142.8 0.8 copy-done.6
  143.6 2.2 %merge.6 = bf16[128,1444]{1,0:T(8,128)(2,1)} custom-call(bf16[192,128]{1,0:T(8,128)(2,1)} %get-tuple-element.114.hot_ref, bf16[8,1,24,1444]{3,2,1,0:T(8,128)(2,1)} %copy-done.6), custom_call_target="tpu_custom_call" | custom-call | flops 1048576 | bytes 65536 | tf_op jit(solution)/shard_map/merge/pallas_call | solution.py:180
  145.8 1.2 collective-permute-start.7
  147.0 4.2 %all-to-all-start.6 = ((bf16[8,1,24,1444]{3,2,1,0:T(8,128)(2,1)}), bf16[8,1,24,1444]{3,2,1,0:T(8,128)(2,1)S(1)}, u32[]{:S(2)}, u32[]{:S(2)}) async-start(bf16[8,1,24,1444]{3,2,1,0:T(8,128)(2,1)} %get-tuple-element.138), calls=%async_computation.6 | async-start | bytes 1179648 | tf_op jit(solution)/shard_map/all_to_all | solution.py:248
  151.2 8.6 %weight_grads.3 = bf16[1,1440,1440]{2,1,0:T(8,128)(2,1)} custom-call(bf16[192,1440]{1,0:T(8,128)(2,1)} %get-tuple-element.145.refs_0_, bf16[192,1440]{1,0:T(8,128)(2,1)} %get-tuple-element.146.refs_1_, bf16[192,1440]{1,0:T(8,128)(2,1)} %get-tuple-element.147.refs_2_, bf16[192,1440]{1,0:T(8,128)(2,1)} %get-tuple-element.148.refs_3_, ...), custom_call_target="tpu_custom_call" | custom-call | flops 12000000000 | bytes 1048576 | tf_op jit(solution)/shard_map/weight_grads/pallas_call | solution.py:222
  159.8 5.7 %collective-permute-done.7.refs_2_ = bf16[128,1444]{1,0:T(8,128)(2,1)S(1)} collective-permute-done((bf16[128,1444]{1,0:T(8,128)(2,1)}, bf16[128,1444]{1,0:T(8,128)(2,1)S(1)}, u32[]{:S(2)}, u32[]{:S(2)}) %collective-permute-start.7) | collective-permute-done | bytes 369696 | tf_op jit(solution)/shard_map/ppermute | solution.py:245
  165.6 0.7 copy-done.9
  166.3 0.2 copy-done.5
  166.5 2.6 %merge.7 = (bf16[1440,128]{1,0:T(8,128)(2,1)}, bf16[4,128]{1,0:T(4,128)(2,1)}) custom-call(bf16[192,128]{1,0:T(8,128)(2,1)} %get-tuple-element.79.hot_ref, bf16[8,1,24,1444]{3,2,1,0:T(8,128)(2,1)} %copy-done.5, bf16[128,1444]{1,0:T(8,128)(2,1)} %copy-done.7, bf16[128,1444]{1,0:T(8,128)(2,1)} %copy-done.8, bf16[128,1444]{1,0:T(8,128)(2,1)} %copy-done.9), custom_call_target="tpu_custom_call" | custom-call | flops 1048576 | bytes 65536 | tf_op jit(solution)/shard_map/merge/pallas_call | solution.py:180
  (22 shorter events, 0.0 us)
Async XLA Ops:
  2.7 20.4 %collective-permute-start.1 = (bf16[2896,128]{1,0:T(8,128)(2,1)}, bf16[2896,128]{1,0:T(8,128)(2,1)S(1)}, u32[]{:S(2)}, u32[]{:S(2)}) collective-permute-start(bf16[2896,128]{1,0:T(8,128)(2,1)} %pack.1.refs_0_), channel_id=1, source_target_pairs={{1,2},{2,1},{5,6},{6,5},{9,10},{10,9},{13,14},{14,13},{17,18},{18,... | collective-permute-start | bytes 2224136 | tf_op jit(solution)/shard_map/ppermute | solution.py:245
  6.2 18.4 %collective-permute-start = (bf16[2896,128]{1,0:T(8,128)(2,1)}, bf16[2896,128]{1,0:T(8,128)(2,1)}, u32[]{:S(2)}, u32[]{:S(2)}) collective-permute-start(bf16[2896,128]{1,0:T(8,128)(2,1)} %pack.1.refs_0_), channel_id=1, source_target_pairs={{0,1},{1,0},{2,3},{3,2},{4,5},{5,4},{6,7},{7,6},{8,9},{9,8},{10,11... | collective-permute-start | bytes 2224136 | tf_op jit(solution)/shard_map/ppermute | solution.py:245
  9.6 22.3 %all-to-all-start = ((bf16[8,24,2976]{2,1,0:T(8,128)(2,1)}), bf16[8,24,2976]{2,1,0:T(8,128)(2,1)S(1)}, u32[]{:S(2)}, u32[]{:S(2)}) async-start(bf16[8,24,2976]{2,1,0:T(8,128)(2,1)} %get-tuple-element.80), calls=%async_computation | async-start | bytes 2359296 | tf_op jit(solution)/shard_map/all_to_all | solution.py:248
  23.1 8.8 %copy-start.10 = (bf16[2896,128]{1,0:T(8,128)(2,1)}, bf16[2896,128]{1,0:T(8,128)(2,1)S(1)}, u32[]{:S(2)}) copy-start(bf16[2896,128]{1,0:T(8,128)(2,1)S(1)} %collective-permute-done.1.refs_0_) | copy-start | bytes 2224132
  24.6 24.6 %collective-permute-start.2 = (bf16[2896,128]{1,0:T(8,128)(2,1)}, bf16[2896,128]{1,0:T(8,128)(2,1)}, u32[]{:S(2)}, u32[]{:S(2)}) collective-permute-start(bf16[2896,128]{1,0:T(8,128)(2,1)} %collective-permute-done.refs_0_), channel_id=1, source_target_pairs={{1,2},{2,1},{5,6},{6,5},{9,10},{10,9},{13,14},{14,13},{17,18},{18,... | collective-permute-start | bytes 2224136 | tf_op jit(solution)/shard_map/ppermute | solution.py:245
  26.9 22.3 %collective-permute-start.3 = (bf16[2896,128]{1,0:T(8,128)(2,1)S(1)}, bf16[2896,128]{1,0:T(8,128)(2,1)}, u32[]{:S(2)}, u32[]{:S(2)}) collective-permute-start(bf16[2896,128]{1,0:T(8,128)(2,1)S(1)} %collective-permute-done.1.refs_0_), channel_id=1, source_target_pairs={{1,0},{2,3},{5,4},{6,7},{9,8},{10,11},{13,12},{14,15},{17,16},{18,... | collective-permute-start | bytes 2224136 | tf_op jit(solution)/shard_map/ppermute | solution.py:245
  31.9 1.0 copy-start.2
  33.0 21.2 %all-to-all-start.1 = ((bf16[8,24,2976]{2,1,0:T(8,128)(2,1)}), bf16[8,24,2976]{2,1,0:T(8,128)(2,1)S(1)}, u32[]{:S(2)}, u32[]{:S(2)}) async-start(bf16[8,24,2976]{2,1,0:T(8,128)(2,1)} %get-tuple-element.84), calls=%async_computation.1 | async-start | bytes 2359296 | tf_op jit(solution)/shard_map/all_to_all | solution.py:248
  49.2 22.2 %collective-permute-start.4 = (bf16[2896,128]{1,0:T(8,128)(2,1)}, bf16[2896,128]{1,0:T(8,128)(2,1)S(1)}, u32[]{:S(2)}, u32[]{:S(2)}) collective-permute-start(bf16[2896,128]{1,0:T(8,128)(2,1)} %collective-permute-done.2.refs_0_), channel_id=1, source_target_pairs={{1,0},{2,3},{5,4},{6,7},{9,8},{10,11},{13,12},{14,15},{17,16},{18,... | collective-permute-start | bytes 2224136 | tf_op jit(solution)/shard_map/ppermute | solution.py:245
  54.2 1.0 copy-start.3
  55.2 20.1 %all-to-all-start.2 = ((bf16[8,24,2976]{2,1,0:T(8,128)(2,1)}), bf16[8,24,2976]{2,1,0:T(8,128)(2,1)S(1)}, u32[]{:S(2)}, u32[]{:S(2)}) async-start(bf16[8,24,2976]{2,1,0:T(8,128)(2,1)} %get-tuple-element.95), calls=%async_computation.2 | async-start | bytes 2359296 | tf_op jit(solution)/shard_map/all_to_all | solution.py:248
  71.4 0.9 copy-start.11
  75.3 1.0 copy-start.1
  76.3 19.7 %all-to-all-start.3 = ((bf16[8,24,2976]{2,1,0:T(8,128)(2,1)}), bf16[8,24,2976]{2,1,0:T(8,128)(2,1)S(1)}, u32[]{:S(2)}, u32[]{:S(2)}) async-start(bf16[8,24,2976]{2,1,0:T(8,128)(2,1)} %get-tuple-element.104), calls=%async_computation.3 | async-start | bytes 2359296 | tf_op jit(solution)/shard_map/all_to_all | solution.py:248
  96.1 1.0 copy-start.4
  97.1 20.3 %all-to-all-start.4 = ((bf16[8,2,24,1444]{3,2,1,0:T(8,128)(2,1)}), bf16[8,2,24,1444]{3,2,1,0:T(8,128)(2,1)S(1)}, u32[]{:S(2)}, u32[]{:S(2)}) async-start(bf16[8,2,24,1444]{3,2,1,0:T(8,128)(2,1)} %get-tuple-element.112), calls=%async_computation.4 | async-start | bytes 2359296 | tf_op jit(solution)/shard_map/all_to_all | solution.py:248
  117.4 1.0 copy-start
  120.8 26.2 %collective-permute-start.5 = (bf16[128,1444]{1,0:T(8,128)(2,1)}, bf16[128,1444]{1,0:T(8,128)(2,1)S(1)}, u32[]{:S(2)}, u32[]{:S(2)}) collective-permute-start(bf16[128,1444]{1,0:T(8,128)(2,1)} %merge.4), channel_id=1, source_target_pairs={{0,1},{1,0},{2,3},{3,2},{4,5},{5,4},{6,7},{7,6},{8,9},{9,8},{10,11... | collective-permute-start | bytes 1109000 | tf_op jit(solution)/shard_map/ppermute | solution.py:245
  123.1 23.8 %collective-permute-start.6 = (bf16[128,1444]{1,0:T(8,128)(2,1)}, bf16[128,1444]{1,0:T(8,128)(2,1)S(1)}, u32[]{:S(2)}, u32[]{:S(2)}) collective-permute-start(bf16[128,1444]{1,0:T(8,128)(2,1)} %merge.5), channel_id=1, source_target_pairs={{0,2},{1,3},{2,0},{3,1},{4,6},{5,7},{6,4},{7,5},{8,10},{9,11},{10,... | collective-permute-start | bytes 1109000 | tf_op jit(solution)/shard_map/ppermute | solution.py:245
  125.4 17.3 %all-to-all-start.5 = ((bf16[8,1,24,1444]{3,2,1,0:T(8,128)(2,1)}), bf16[8,1,24,1444]{3,2,1,0:T(8,128)(2,1)S(1)}, u32[]{:S(2)}, u32[]{:S(2)}) async-start(bf16[8,1,24,1444]{3,2,1,0:T(8,128)(2,1)} %get-tuple-element.121), calls=%async_computation.5 | async-start | bytes 1179648 | tf_op jit(solution)/shard_map/all_to_all | solution.py:248
  142.8 0.8 copy-start.6
  145.8 19.8 %collective-permute-start.7 = (bf16[128,1444]{1,0:T(8,128)(2,1)}, bf16[128,1444]{1,0:T(8,128)(2,1)S(1)}, u32[]{:S(2)}, u32[]{:S(2)}) collective-permute-start(bf16[128,1444]{1,0:T(8,128)(2,1)} %merge.6), channel_id=1, source_target_pairs={{0,3},{1,2},{2,1},{3,0},{4,7},{5,6},{6,5},{7,4},{8,11},{9,10},{10,... | collective-permute-start | bytes 1109000 | tf_op jit(solution)/shard_map/ppermute | solution.py:245
  146.9 12.9 %copy-start.7 = (bf16[128,1444]{1,0:T(8,128)(2,1)}, bf16[128,1444]{1,0:T(8,128)(2,1)S(1)}, u32[]{:S(2)}) copy-start(bf16[128,1444]{1,0:T(8,128)(2,1)S(1)} %collective-permute-done.5.refs_0_) | copy-start | bytes 1108996
  146.9 12.9 %copy-start.8 = (bf16[128,1444]{1,0:T(8,128)(2,1)}, bf16[128,1444]{1,0:T(8,128)(2,1)S(1)}, u32[]{:S(2)}) copy-start(bf16[128,1444]{1,0:T(8,128)(2,1)S(1)} %collective-permute-done.6.refs_1_) | copy-start | bytes 1108996
  147.0 18.6 %all-to-all-start.6 = ((bf16[8,1,24,1444]{3,2,1,0:T(8,128)(2,1)}), bf16[8,1,24,1444]{3,2,1,0:T(8,128)(2,1)S(1)}, u32[]{:S(2)}, u32[]{:S(2)}) async-start(bf16[8,1,24,1444]{3,2,1,0:T(8,128)(2,1)} %get-tuple-element.138), calls=%async_computation.6 | async-start | bytes 1179648 | tf_op jit(solution)/shard_map/all_to_all | solution.py:248
  165.6 0.8 copy-start.9
  165.6 0.9 copy-start.5
where the time goes:
time: 171 us; the launch traced here: 169 us
  Pallas kernels  92.3 us (54%)
  starting transfers between devices  44.9 us (26%)
  waiting for transfers between devices  22.7 us (13%)
  local copies, waits for them, and re-layouts  7.72 us (5%)
    pallas_call x4, Pallas kernels, expert(): pl.pallas_call(functools.partial(expert_kernel, width, hidden, lane, topk...  48.3 us
    all_to_all x7, starting transfers between devices, a2a(): return lax.all_to_all(v, 'island', 0, 0, tiled=True)  31.4 us
    pallas_call x2, Pallas kernels, weight_grads(): pl.pallas_call(functools.partial(weights_kernel, [len(v) for v in (left,...  21 us
    ppermute x8, waiting for transfers between devices, send(): return lax.ppermute(v, 'local', pairs)  16.4 us
    ppermute x8, starting transfers between devices, send(): return lax.ppermute(v, 'local', pairs)  13.6 us
    pallas_call x4, Pallas kernels, pick(): pl.pallas_call(functools.partial(pick_kernel, width, meta, lane, islands,...  11.5 us
    pallas_call x4, Pallas kernels, merge(): pl.pallas_call(functools.partial(merge_kernel, topk, at), out_shape=[jax....  9.5 us
    unnamed x24, local copies, waits for them, and re-layouts  7.72 us
  transfers between devices with their start and end apart: 15, of which 5 were waited for; matrix products, arithmetic and copies ran while one was open for 0% of the time, Pallas kernels for 50%

commit v1 on v0

--- a/solution.py
+++ b/solution.py
@@ -50,7 +50,7 @@
 HBM = pl.BlockSpec(memory_space=pl.ANY)
 COST = pl.CostEstimate(flops=1 << 20, transcendentals=0, bytes_accessed=1 << 16)
 LONG = pl.CostEstimate(flops=12_000_000_000, transcendentals=0, bytes_accessed=1 << 20)
-GRANT = pltpu.CompilerParams(vmem_limit_bytes=56 << 20)
+GRANT = pltpu.CompilerParams(vmem_limit_bytes=63 << 20)
 
 
 def slots_of(ids, experts, cap):
@@ -94,8 +94,9 @@
     )(place, *blocks)
 
 
-def expert_kernel(width, hidden, lane, topk, n, step, place_ref, got_ref, wg_hbm, wu_hbm, wd_hbm, *refs):
-    prev, ret_ref, ys_ref, a_ref, dh_ref, du_ref, wg, wu, wd, h_ref, u_ref, sems = (None,) * (12 - len(refs)) + refs
+def expert_kernel(width, hidden, lane, topk, n, step, fan, place_ref, got_ref, wg_hbm, wu_hbm, wd_hbm, *refs):
+    wg, wu, wd, h_ref, u_ref, sems, back_ref = refs[len(refs) - 7:]
+    *ahead, ys_ref, a_ref, dh_ref, du_ref = refs[:len(refs) - 7]
     loads = [pltpu.make_async_copy(src, dst, sems.at[i])
              for i, (src, dst) in enumerate(((wg_hbm, wg), (wu_hbm, wu), (wd_hbm, wd)))]
     for load in loads:
@@ -130,35 +131,41 @@
         dh_ref[:, cut] = (da * u * sig * (1.0 + h * (1.0 - sig))).astype(BF)
         du_ref[:, cut] = (da * act).astype(BF)
     dh, du = dh_ref[...], du_ref[...]
-    islands, depth, cap, _ = ret_ref.shape
-    if prev is not None:
-        ret_ref[:, :depth - 1] = prev[...]
     for at, size in tiles(width, step):
         cut = slice(at, at + size)
-        dx = dot(dh, wg[cut, :], 1, 1) + dot(du, wu[cut, :], 1, 1)
-        ret_ref[:, depth - 1, :, cut] = dx.reshape(islands, cap, size).astype(BF)
-    ret_ref[:, depth - 1, :, width:] = jnp.where(mine, gp, 0.0).reshape(islands, cap, topk).astype(BF)
-
-
-def expert(place, got, wg, wu, wd, width, lane, topk, n, islands, prev=None):
+        back_ref[:, cut] = dot(dh, wg[cut, :], 1, 1) + dot(du, wu[cut, :], 1, 1)
+    back_ref[:, width:] = jnp.where(mine, gp, 0.0)
+    if fan:
+        for j, ret_ref in enumerate(ahead):
+            cap = ret_ref.shape[0]
+            at = pl.multiple_of((place_ref[0] ^ j) * cap, 8)
+            ret_ref[...] = back_ref[pl.ds(at, cap), :].astype(BF)
+        return
+    ret_ref = ahead[-1]
+    islands, depth, cap, cols = ret_ref.shape
+    if depth > 1:
+        ret_ref[:, :depth - 1] = ahead[0][...]
+    ret_ref[:, depth - 1] = back_ref[...].reshape(islands, cap, cols).astype(BF)
+
+
+def expert(place, got, wg, wu, wd, width, lane, topk, n, islands, prev=None, fan=False):
     rows, hidden = got.shape[0], wg.shape[1]
     depth = 1 if prev is None else prev.shape[1] + 1
     cols = (width, hidden, hidden, hidden)
     before = [] if prev is None else [prev]
+    shape = (rows // islands, width + topk)
+    back = [shape] * islands if fan else [(islands, depth) + shape]
     outs = pl.pallas_call(
-        functools.partial(expert_kernel, width, hidden, lane, topk, n, 384),
-        out_shape=[jax.ShapeDtypeStruct((islands, depth, rows // islands, width + topk), BF)]
-        + [jax.ShapeDtypeStruct((rows, c), BF) for c in cols],
+        functools.partial(expert_kernel, width, hidden, lane, topk, n, 512, fan),
+        out_shape=[jax.ShapeDtypeStruct(o, BF) for o in back + [(rows, c) for c in cols]],
         in_specs=[SMEM, VMEM] + [HBM] * 3 + [VMEM] * len(before),
-        out_specs=[VMEM] * 5,
+        out_specs=[VMEM] * (len(back) + 4),
         scratch_shapes=[pltpu.VMEM(wg.shape, BF), pltpu.VMEM(wu.shape, BF), pltpu.VMEM(wd.shape, BF),
                         pltpu.VMEM((rows, hidden), F32), pltpu.VMEM((rows, hidden), F32),
-                        pltpu.SemaphoreType.DMA((3,))],
-        compiler_params=GRANT,
-        cost_estimate=COST,
-        name="expert",
+                        pltpu.SemaphoreType.DMA((3,)), pltpu.VMEM((rows, width + topk), F32)],
+        compiler_params=GRANT, cost_estimate=COST, name="expert",
     )(place, got, wg, wu, wd, *before)
-    return outs[0], outs[1:]
+    return (outs[:islands] if fan else outs[0]), outs[len(back):]
 
 
 def merge_kernel(topk, at, hot_ref, back_ref, *refs):
@@ -174,6 +181,25 @@
     refs[-1][...] = total[:, cols - topk:].T.astype(BF)
 
 
+def gather_kernel(place_ref, hot_ref, *refs):
+    backs, out_ref, rows_ref = refs[:-2], refs[-2], refs[-1]
+    for j, back in enumerate(backs):
+        cap = back.shape[0]
+        at = pl.multiple_of((place_ref[0] ^ j) * cap, 8)
+        rows_ref[pl.ds(at, cap), :] = back[...].astype(F32)
+    out_ref[...] = dot(hot_ref[...], rows_ref[...].astype(BF), 0, 0).astype(BF)
+
+
+def gather(place, hot, backs):
+    cols = backs[0].shape[1]
+    return pl.pallas_call(
+        gather_kernel, out_shape=jax.ShapeDtypeStruct((hot.shape[1], cols), BF),
+        in_specs=[SMEM] + [VMEM] * (1 + len(backs)), out_specs=VMEM,
+        scratch_shapes=[pltpu.VMEM((hot.shape[0], cols), F32)],
+        compiler_params=GRANT, cost_estimate=COST, name="gather",
+    )(place, hot, *backs)
+
+
 def merge(hot, back, at, topk, others=()):
     cols, tokens = back.shape[3], hot.shape[1]
     outs = [(cols - topk, tokens), (topk, tokens)] if others else [(tokens, cols)]
@@ -186,23 +212,26 @@
     return res if others else res[0]
 
 
-def pack_kernel(acts_ref, probs_ref, ids_ref, grad_ref, out_ref):
-    width, topk = acts_ref.shape[0], ids_ref.shape[0]
-    meta = out_ref.shape[0] - 2 * width
+def pack_kernel(width, meta, lane, islands, n, cap, topk, place_ref, acts_ref, probs_ref, ids_ref, grad_ref,
+                own_ref, out_ref, hot_ref):
     label = jnp.concatenate(
         [probs_ref[...].astype(F32), ids_ref[...].astype(F32),
          jnp.zeros((meta - 2 * topk, ids_ref.shape[1]), F32)], axis=0)
-    out_ref[:width, :] = acts_ref[...]
-    out_ref[width:width + meta, :] = label.astype(BF)
-    out_ref[width + meta:, :] = grad_ref[...]
-
-
-def pack(acts, probs, ids, grad, meta):
-    width, tokens = acts.shape
+    own_ref[:width, :] = acts_ref[...]
+    own_ref[width:width + meta, :] = label.astype(BF)
+    own_ref[width + meta:, :] = grad_ref[...]
+    pick_kernel(width, meta, lane, islands, n, cap, topk, place_ref, own_ref, out_ref, hot_ref)
+
+
+def pack(place, acts, probs, ids, grad, width, meta, lane, islands, n, cap, topk):
+    tokens = acts.shape[1]
     return pl.pallas_call(
-        pack_kernel, out_shape=jax.ShapeDtypeStruct((2 * width + meta, tokens), BF),
-        in_specs=[VMEM] * 4, out_specs=VMEM, compiler_params=GRANT, cost_estimate=COST, name="pack",
-    )(acts, probs, ids, grad)
+        functools.partial(pack_kernel, width, meta, lane, islands, n, cap, topk),
+        out_shape=[jax.ShapeDtypeStruct((2 * width + meta, tokens), BF),
+                   jax.ShapeDtypeStruct((islands, cap, lane + width), BF),
+                   jax.ShapeDtypeStruct((islands * cap, tokens), BF)],
+        in_specs=[SMEM] + [VMEM] * 4, out_specs=[VMEM] * 3, compiler_params=GRANT, cost_estimate=COST, name="pack",
+    )(place, acts, probs, ids, grad)
 
 
 def weights_kernel(counts, *refs):
@@ -210,22 +239,29 @@
     for count in counts:
         stacks.append(jnp.concatenate([r[...] for r in refs[at:at + count]], axis=0))
         at += count
-    for right, out in zip(stacks[1:], refs[at:]):
-        out[0] = dot(stacks[0], right, 0, 0).astype(BF)
-
-
-def weight_grads(left, rights, width, step=256):
-    rows = sum(v.shape[0] for v in left)
-    cols = [pl.BlockSpec((v.shape[0], step), lambda i: (0, i)) for v in left]
-    full = [pl.BlockSpec(v.shape, lambda i: (0, 0)) for right in rights for v in right]
-    outs = [right[0].shape[1] for right in rights]
+    gg_ref, gu_ref, gd_ref = refs[at:]
+    x, dh, du, a, ys = stacks
+    gg_ref[0] = dot(x, dh, 0, 0).astype(BF)
+    gu_ref[0] = dot(x, du, 0, 0).astype(BF)
+    gd_ref[0] = dot(a, ys, 0, 0).astype(BF)
+
+
+def weight_grads(x, dh, du, a, ys, step=256):
+    width, hidden = ys[0].shape[1], a[0].shape[1]
+    rows = sum(v.shape[0] for v in x)
+    cols = lambda vs: [pl.BlockSpec((v.shape[0], step), lambda i: (0, i)) for v in vs]
+    full = lambda vs: [pl.BlockSpec(v.shape, lambda i: (0, 0)) for v in vs]
+    outs = [(width, hidden), (width, hidden), (hidden, width)]
     return pl.pallas_call(
-        functools.partial(weights_kernel, [len(v) for v in (left, *rights)]), grid=(pl.cdiv(width, step),),
-        out_shape=[jax.ShapeDtypeStruct((1, width, o), BF) for o in outs],
-        in_specs=cols + full,
-        out_specs=[pl.BlockSpec((1, step, o), lambda i: (0, i, 0)) for o in outs],
-        compiler_params=GRANT, cost_estimate=LONG, name="weight_grads",
-    )(*left, *[v for right in rights for v in right])
+        functools.partial(weights_kernel, [len(v) for v in (x, dh, du, a, ys)]),
+        grid=(pl.cdiv(max(width, hidden), step),),
+        out_shape=[jax.ShapeDtypeStruct((1,) + o, BF) for o in outs],
+        in_specs=cols(x) + full(dh) + full(du) + cols(a) + full(ys),
+        out_specs=[pl.BlockSpec((1, step, o[1]), lambda i: (0, i, 0)) for o in outs],
+        compiler_params=GRANT,
+        cost_estimate=LONG,
+        name="weight_grads",
+    )(*x, *dh, *du, *a, *ys)
 
 
 def line_of_four(acts, grad_out, expert_ids, route_probs, wg, wu, wd):
@@ -253,16 +289,20 @@
     def deal(rows):
         return a2a(rows).reshape(islands * cap, -1)
 
-    def work(got, prev=None):
-        return expert(place, got, wg, wu, wd, width, lane, topk, n, islands, prev)
+    def work(got, prev=None, fan=False):
+        return expert(place, got, wg, wu, wd, width, lane, topk, n, islands, prev, fan)
+
+    def give(rets):
+        return [rets[0]] + [lax.ppermute(rets[j], "island", [(i, i ^ j) for i in range(islands)])
+                            for j in range(1, islands)]
 
     def part(total, s):
         return send(total, [(i, i ^ s) for i in range(n)])
 
-    own = pack(acts.T, route_probs.T, expert_ids.T, grad_out.T, meta)
-    rows0, hot0 = take(own)
+    own, rows0, hot0 = pack(place, acts.T, route_probs.T, expert_ids.T, grad_out.T,
+                            width, meta, lane, islands, n, cap, topk)
     got0 = deal(rows0)
-    one, near, rows0 = seal((send(own, outer), send(own, middle), rows0))
+    one, near = seal((send(own, outer), send(own, middle)))
     two_in, two_out = send(one, middle), send(near, ends)
     rows1, hot1 = take(one)
     got0, rows1 = seal((got0, rows1))
@@ -273,28 +313,31 @@
     rows2, hot2 = take(two_in, two_out)
     got1, rows2, keep0 = seal((got1, rows2, keep0))
     got2 = deal(rows2)
-    ret1, keep1 = work(got1)
-    three, ret1 = seal((three, ret1))
+    ret01, keep1 = work(got1, ret0)
+    three, ret01 = seal((three, ret01))
     rows3, hot3 = take(near, three)
     got2, rows3, keep1 = seal((got2, rows3, keep1))
     got3 = deal(rows3)
-    ret12, keep2 = work(got2, ret1)
-    got3, ret12, keep2 = seal((got3, ret12, keep2))
-    back12 = a2a(ret12)
-    ret3, keep3 = work(got3)
-    merge1, merge2 = merge(hot1, back12, 0, topk), merge(hot2, back12, 1, topk)
-    part1, part2 = part(merge1, 1), part(merge2, 2)
-    merge1, merge2, ret3, keep3 = seal((merge1, merge2, ret3, keep3))
-    back3 = a2a(ret3)
+    ret2, keep2 = work(got2, fan=True)
+    back2 = give(ret2)
+    got3, keep2, back2 = seal((got3, keep2, back2))
+    merge2 = gather(place, hot2, back2)
+    part2 = part(merge2, 2)
+    merge2, ret01, got3 = seal((merge2, ret01, got3))
+    back01 = a2a(ret01)
+    ret3, keep3 = work(got3, fan=True)
+    back3 = give(ret3)
+    back01, keep3 = seal((back01, keep3))
+    merge1 = merge(hot1, back01, 1, topk)
+    part1 = part(merge1, 1)
+    merge1, back3 = seal((merge1, back3))
+    merge3 = gather(place, hot3, back3)
+    part3 = part(merge3, 3)
+    part2, merge3, keep3 = seal((part2, merge3, keep3))
     ys, a, dh, du = zip(keep0, keep1, keep2, keep3)
-    gg, gu = weight_grads((got0, got1, got2, got3), (dh, du), width)
-    back3, gg, ret0 = seal((back3, gg, ret0))
-    merge3 = merge(hot3, back3, 0, topk)
-    part3 = part(merge3, 3)
-    part1, part2, merge3, ret0, a = seal((part1, part2, merge3, ret0, a))
-    back0 = a2a(ret0)
-    gd, = weight_grads(a, (ys,), wd.shape[0])
-    grad_in, grad_probs = merge(hot0, back0, 0, topk, (part1, part2, part3))
+    gg, gu, gd = weight_grads((got0, got1, got2, got3), dh, du, a, ys)
+    part1, part2, gg = seal((part1, part2, gg))
+    grad_in, grad_probs = merge(hot0, back01, 0, topk, (part1, part2, part3))
     return grad_in.T, grad_probs.T, gg, gu, gd
 
 

time: 171 us -> 164 us (0.959)
  the two profiles are of different devices: /device:TPU:10 before, /device:TPU:1 now
where the time goes in v1:
time: 164 us; the launch traced here: 161 us
  Pallas kernels  84.7 us (52%)
  starting transfers between devices  57.8 us (35%)
  waiting for transfers between devices  16 us (10%)
    pallas_call x4, Pallas kernels, expert(): pl.pallas_call(functools.partial(expert_kernel, width, hidden, lane, topk...  46.1 us
    all_to_all x5, starting transfers between devices, a2a(): return lax.all_to_all(v, 'island', 0, 0, tiled=True)  26.5 us
    pallas_call x1, Pallas kernels, weight_grads(): pl.pallas_call(functools.partial(weights_kernel, [len(v) for v in (x, dh,...  17.4 us
    ppermute x14, starting transfers between devices, give(): lax.ppermute(rets[j], 'island', [(i, i ^ j) for i in range(islands)])  16.6 us
    ppermute x8, starting transfers between devices, send(): return lax.ppermute(v, 'local', pairs)  14.8 us
    ppermute x8, waiting for transfers between devices, send(): return lax.ppermute(v, 'local', pairs)  11.2 us
    pallas_call x3, Pallas kernels, pick(): pl.pallas_call(functools.partial(pick_kernel, width, meta, lane, islands,...  8.71 us
    pallas_call x2, Pallas kernels, merge(): pl.pallas_call(functools.partial(merge_kernel, topk, at), out_shape=[jax....  5.18 us
  transfers between devices with their start and end apart: 27, of which 6 were waited for; matrix products, arithmetic and copies ran while one was open for 0% of the time, Pallas kernels for 48%

profile of v1, /device:TPU:1, one launch (start us, length us, event | category | flops | bytes accessed | tf_op | source)
XLA Modules:
  0.0 161.5 jit_solution(9597120807302962900)
XLA Ops:
  0.6 0.6 pad_add_fusion.place_ref
  1.3 2.8 %pack.1 = (bf16[2896,128]{1,0:T(8,128)(2,1)}, bf16[8,24,2976]{2,1,0:T(8,128)(2,1)}, bf16[192,128]{1,0:T(8,128)(2,1)}) custom-call(s32[3]{0:T(128)} %pad_add_fusion.place_ref, bf16[1440,128]{1,0:T(8,128)(2,1)} %bitcast.28, bf16[4,128]{1,0:T(4,128)(2,1)} %bitcast.31, s32[4,128]{1,0:T(4,128)} %bitcast.30, bf16[1440,128]{1,0:T(8,128)(2,1)} %bitcast.29), custom_call_target="tpu_custom_call" | custom-call | flops 1048576 | bytes 65536 | tf_op jit(solution)/shard_map/pack/pallas_call | solution.py:228
  4.0 0.7 collective-permute-start.1
  4.7 4.7 %collective-permute-start = (bf16[2896,128]{1,0:T(8,128)(2,1)}, bf16[2896,128]{1,0:T(8,128)(2,1)}, u32[]{:S(2)}, u32[]{:S(2)}) collective-permute-start(bf16[2896,128]{1,0:T(8,128)(2,1)} %get-tuple-element.111), channel_id=1, source_target_pairs={{0,1},{1,0},{2,3},{3,2},{4,5},{5,4},{6,7},{7,6},{8,9},{9,8},{10,11... | collective-permute-start | bytes 2224136 | tf_op jit(solution)/shard_map/ppermute | solution.py:281
  9.4 5.4 %all-to-all-start = ((bf16[8,24,2976]{2,1,0:T(8,128)(2,1)}), bf16[8,24,2976]{2,1,0:T(8,128)(2,1)}, u32[]{:S(2)}, u32[]{:S(2)}) async-start(bf16[8,24,2976]{2,1,0:T(8,128)(2,1)} %get-tuple-element.114), calls=%async_computation | async-start | bytes 2359296 | tf_op jit(solution)/shard_map/all_to_all | solution.py:284
  14.8 10.9 %collective-permute-done.refs_0_ = bf16[2896,128]{1,0:T(8,128)(2,1)} collective-permute-done((bf16[2896,128]{1,0:T(8,128)(2,1)}, bf16[2896,128]{1,0:T(8,128)(2,1)}, u32[]{:S(2)}, u32[]{:S(2)}) %collective-permute-start) | collective-permute-done | bytes 741408 | tf_op jit(solution)/shard_map/ppermute | solution.py:281
  25.7 1.5 collective-permute-start.2
  27.3 1.3 collective-permute-start.3
  28.6 2.8 %pick.3 = (bf16[8,24,2976]{2,1,0:T(8,128)(2,1)}, bf16[192,128]{1,0:T(8,128)(2,1)}) custom-call(s32[3]{0:T(128)} %pad_add_fusion.place_ref, bf16[2896,128]{1,0:T(8,128)(2,1)} %collective-permute-done.refs_0_), custom_call_target="tpu_custom_call" | custom-call | flops 12000000000 | bytes 1048576 | tf_op jit(solution)/shard_map/pick/pallas_call | solution.py:88
  31.3 5.7 %all-to-all-start.1 = ((bf16[8,24,2976]{2,1,0:T(8,128)(2,1)}), bf16[8,24,2976]{2,1,0:T(8,128)(2,1)}, u32[]{:S(2)}, u32[]{:S(2)}) async-start(bf16[8,24,2976]{2,1,0:T(8,128)(2,1)} %get-tuple-element.121), calls=%async_computation.1 | async-start | bytes 2359296 | tf_op jit(solution)/shard_map/all_to_all | solution.py:284
  37.0 11.3 %expert.4 = (bf16[8,1,24,1444]{3,2,1,0:T(8,128)(2,1)}, bf16[192,1440]{1,0:T(8,128)(2,1)}, bf16[192,1440]{1,0:T(8,128)(2,1)}, bf16[192,1440]{1,0:T(8,128)(2,1)}, bf16[192,1440]{1,0:T(8,128)(2,1)}) custom-call(s32[3]{0:T(128)} %pad_add_fusion.place_ref, bf16[192,2976]{1,0:T(8,128)(2,1)} %bitcast.7.got_ref.refs_0_, bf16[1440,1440]{1,0:T(8,128)(2,1)} %bitcast.16, ...), custom_call_target="tpu_custom_call" | custom-call | flops 1048576 | bytes 65536 | tf_op jit(solution)/shard_map/expert/pallas_call | solution.py:158
  48.4 1.3 collective-permute-start.4
  49.7 3.0 %pick.4 = (bf16[8,24,2976]{2,1,0:T(8,128)(2,1)}, bf16[192,128]{1,0:T(8,128)(2,1)}) custom-call(s32[3]{0:T(128)} %pad_add_fusion.place_ref, bf16[2896,128]{1,0:T(8,128)(2,1)} %collective-permute-done.2.refs_0_, bf16[2896,128]{1,0:T(8,128)(2,1)} %collective-permute-done.3.refs_1_), custom_call_target="tpu_custom_call" | custom-call | flops 12000000000 | bytes 1048576 | tf_op jit(solution)/shard_map/pick/pallas_call | solution.py:88
  52.7 5.4 %all-to-all-start.2 = ((bf16[8,24,2976]{2,1,0:T(8,128)(2,1)}), bf16[8,24,2976]{2,1,0:T(8,128)(2,1)}, u32[]{:S(2)}, u32[]{:S(2)}) async-start(bf16[8,24,2976]{2,1,0:T(8,128)(2,1)} %get-tuple-element.127), calls=%async_computation.2 | async-start | bytes 2359296 | tf_op jit(solution)/shard_map/all_to_all | solution.py:284
  58.1 11.7 %expert.5 = (bf16[8,2,24,1444]{3,2,1,0:T(8,128)(2,1)}, bf16[192,1440]{1,0:T(8,128)(2,1)}, bf16[192,1440]{1,0:T(8,128)(2,1)}, bf16[192,1440]{1,0:T(8,128)(2,1)}, bf16[192,1440]{1,0:T(8,128)(2,1)}) custom-call(s32[3]{0:T(128)} %pad_add_fusion.place_ref, bf16[192,2976]{1,0:T(8,128)(2,1)} %bitcast.11.got_ref.refs_1_, bf16[1440,1440]{1,0:T(8,128)(2,1)} %bitcast.17, ...), custom_call_target="tpu_custom_call" | custom-call | flops 1048576 | bytes 65536 | tf_op jit(solution)/shard_map/expert/pallas_call | solution.py:158
  69.8 0.2 collective-permute-done.4.refs_1_
  70.0 0.9 copy-done.12
  70.9 3.0 %pick.5 = (bf16[8,24,2976]{2,1,0:T(8,128)(2,1)}, bf16[192,128]{1,0:T(8,128)(2,1)}) custom-call(s32[3]{0:T(128)} %pad_add_fusion.place_ref, bf16[2896,128]{1,0:T(8,128)(2,1)} %copy-done.11, bf16[2896,128]{1,0:T(8,128)(2,1)} %copy-done.12), custom_call_target="tpu_custom_call" | custom-call | flops 12000000000 | bytes 1048576 | tf_op jit(solution)/shard_map/pick/pallas_call | solution.py:88
  73.9 5.3 %all-to-all-start.3 = ((bf16[8,24,2976]{2,1,0:T(8,128)(2,1)}), bf16[8,24,2976]{2,1,0:T(8,128)(2,1)}, u32[]{:S(2)}, u32[]{:S(2)}) async-start(bf16[8,24,2976]{2,1,0:T(8,128)(2,1)} %get-tuple-element.137), calls=%async_computation.3 | async-start | bytes 2359296 | tf_op jit(solution)/shard_map/all_to_all | solution.py:284
  79.2 11.5 %expert.6 = (bf16[24,1444]{1,0:T(8,128)(2,1)}, bf16[24,1444]{1,0:T(8,128)(2,1)}, bf16[24,1444]{1,0:T(8,128)(2,1)}, bf16[24,1444]{1,0:T(8,128)(2,1)}, bf16[24,144...) custom-call(s32[3]{0:T(128)} %pad_add_fusion.place_ref, ...), custom_call_target="tpu_custom_call" | custom-call | flops 1048576 | bytes 65536 | tf_op jit(solution)/shard_map/expert/pallas_call | solution.py:158
  90.7 0.2 collective-permute-start.5
  90.9 1.6 collective-permute-start.6
  92.6 0.4 collective-permute-start.7
  93.0 1.4 collective-permute-start.8
  94.4 0.3 collective-permute-start.9
  94.6 2.3 %collective-permute-start.10 = (bf16[24,1444]{1,0:T(8,128)(2,1)}, bf16[24,1444]{1,0:T(8,128)(2,1)S(1)}, u32[]{:S(2)}, u32[]{:S(2)}) collective-permute-start(bf16[24,1444]{1,0:T(8,128)(2,1)} %get-tuple-element.149), channel_id=1, source_target_pairs={{0,24},{4,28},{8,16},{12,20},{16,8},{20,12},{24,0},{28,4},{1,25},{... | collective-permute-start | bytes 207944 | tf_op jit(solution)/shard_map/ppermute | solution.py:296
  97.0 1.8 %collective-permute-start.11 = (bf16[24,1444]{1,0:T(8,128)(2,1)}, bf16[24,1444]{1,0:T(8,128)(2,1)S(1)}, u32[]{:S(2)}, u32[]{:S(2)}) collective-permute-start(bf16[24,1444]{1,0:T(8,128)(2,1)} %get-tuple-element.150), channel_id=1, source_target_pairs={{0,28},{4,24},{8,20},{12,16},{16,12},{20,8},{24,4},{28,0},{1,29},{... | collective-permute-start | bytes 207944 | tf_op jit(solution)/shard_map/ppermute | solution.py:296
  98.9 1.6 collective-permute-done.9.refs_5_
  100.4 2.0 %collective-permute-done.11.refs_7_ = bf16[24,1444]{1,0:T(8,128)(2,1)S(1)} collective-permute-done((bf16[24,1444]{1,0:T(8,128)(2,1)}, bf16[24,1444]{1,0:T(8,128)(2,1)S(1)}, u32[]{:S(2)}, u32[]{:S(2)}) %collective-permute-start.11) | collective-permute-done | bytes 69344 | tf_op jit(solution)/shard_map/ppermute | solution.py:296
  102.5 0.6 copy-done.10
  103.1 2.3 %gather.2 = bf16[128,1444]{1,0:T(8,128)(2,1)} custom-call(s32[3]{0:T(128)} %pad_add_fusion.place_ref, bf16[192,128]{1,0:T(8,128)(2,1)} %get-tuple-element.120.hot_ref, bf16[24,1444]{1,0:T(8,128)(2,1)} %get-tuple-element.151.refs_0_, bf16[24,1444]{1,0:T(8,128)(2,1)} %copy-done.4, bf16[24,1444]{1,0:T(8,128)(2,1)} %copy-done.5, bf16[24,1444]{1,0:T(8,128)(2,1)} %copy-done.6, ...), custom_call_target="tpu_custom_call" | custom-call | flops 1048576 | bytes 65536 | tf_op jit(solution)/shard_map/gather/pallas_call | solution.py:195
  105.4 4.7 %all-to-all-start.4 = ((bf16[8,2,24,1444]{3,2,1,0:T(8,128)(2,1)}), bf16[8,2,24,1444]{3,2,1,0:T(8,128)(2,1)}, u32[]{:S(2)}, u32[]{:S(2)}) async-start(bf16[8,2,24,1444]{3,2,1,0:T(8,128)(2,1)} %get-tuple-element.161), calls=%async_computation.4 | async-start | bytes 2359296 | tf_op jit(solution)/shard_map/all_to_all | solution.py:284
  110.0 4.2 %collective-permute-start.13 = (bf16[128,1444]{1,0:T(8,128)(2,1)S(1)}, bf16[128,1444]{1,0:T(8,128)(2,1)S(1)}, u32[]{:S(2)}, u32[]{:S(2)}) collective-permute-start(bf16[128,1444]{1,0:T(8,128)(2,1)S(1)} %copy-done.1), channel_id=1, source_target_pairs={{0,2},{1,3},{2,0},{3,1},{4,6},{5,7},{6,4},{7,5},{8,10},{9,11},{10,... | collective-permute-start | bytes 1109000 | tf_op jit(solution)/shard_map/ppermute | solution.py:281
  114.2 11.6 %expert.7 = (bf16[24,1444]{1,0:T(8,128)(2,1)}, bf16[24,1444]{1,0:T(8,128)(2,1)}, bf16[24,1444]{1,0:T(8,128)(2,1)}, bf16[24,1444]{1,0:T(8,128)(2,1)}, bf16[24,144...) custom-call(s32[3]{0:T(128)} %pad_add_fusion.place_ref, ...), custom_call_target="tpu_custom_call" | custom-call | flops 1048576 | bytes 65536 | tf_op jit(solution)/shard_map/expert/pallas_call | solution.py:158
  125.8 0.8 collective-permute-start.14
  126.6 1.3 collective-permute-start.15
  127.9 0.4 collective-permute-start.16
  128.3 1.3 collective-permute-start.17
  129.6 0.5 collective-permute-start.18
  130.1 0.5 collective-permute-done.15.refs_2_
  130.6 2.3 %collective-permute-start.19 = (bf16[24,1444]{1,0:T(8,128)(2,1)}, bf16[24,1444]{1,0:T(8,128)(2,1)}, u32[]{:S(2)}, u32[]{:S(2)}) collective-permute-start(bf16[24,1444]{1,0:T(8,128)(2,1)} %get-tuple-element.176), channel_id=1, source_target_pairs={{0,24},{4,28},{8,16},{12,20},{16,8},{20,12},{24,0},{28,4},{1,25},{... | collective-permute-start | bytes 207944 | tf_op jit(solution)/shard_map/ppermute | solution.py:296
  132.9 2.0 %collective-permute-start.20 = (bf16[24,1444]{1,0:T(8,128)(2,1)}, bf16[24,1444]{1,0:T(8,128)(2,1)}, u32[]{:S(2)}, u32[]{:S(2)}) collective-permute-start(bf16[24,1444]{1,0:T(8,128)(2,1)} %get-tuple-element.177), channel_id=1, source_target_pairs={{0,28},{4,24},{8,20},{12,16},{16,12},{20,8},{24,4},{28,0},{1,29},{... | collective-permute-start | bytes 207944 | tf_op jit(solution)/shard_map/ppermute | solution.py:296
  134.9 2.4 %merge.2 = bf16[128,1444]{1,0:T(8,128)(2,1)} custom-call(bf16[192,128]{1,0:T(8,128)(2,1)} %get-tuple-element.168.hot_ref, bf16[8,2,24,1444]{3,2,1,0:T(8,128)(2,1)} %all-to-all-done.4.back_ref), custom_call_target="tpu_custom_call" | custom-call | flops 1048576 | bytes 65536 | tf_op jit(solution)/shard_map/merge/pallas_call | solution.py:206
  137.2 0.6 collective-permute-done.20.refs_7_
  137.9 2.3 %gather.3 = bf16[128,1444]{1,0:T(8,128)(2,1)} custom-call(s32[3]{0:T(128)} %pad_add_fusion.place_ref, bf16[192,128]{1,0:T(8,128)(2,1)} %get-tuple-element.169.hot_ref, bf16[24,1444]{1,0:T(8,128)(2,1)} %get-tuple-element.178.refs_0_, bf16[24,1444]{1,0:T(8,128)(2,1)} %copy-done.2, bf16[24,1444]{1,0:T(8,128)(2,1)} %copy-done.3, ...), custom_call_target="tpu_custom_call" | custom-call | flops 1048576 | bytes 65536 | tf_op jit(solution)/shard_map/gather/pallas_call | solution.py:195
  140.1 1.1 collective-permute-start.21
  141.2 17.4 %weight_grads.1 = (bf16[1,1440,1440]{2,1,0:T(8,128)(2,1)}, bf16[1,1440,1440]{2,1,0:T(8,128)(2,1)}, bf16[1,1440,1440]{2,1,0:T(8,128)(2,1)}) custom-call(bf16[192,2976]{1,0:T(8,128)(2,1)} %bitcast.7.got_ref.refs_0_, bf16[192,2976]{1,0:T(8,128)(2,1)} %bitcast.11.got_ref.refs_1_, bf16[192,2976]{1,0:T(8,128)(2,1)} %bitcast.12.got_ref.refs_2_, ...), custom_call_target="tpu_custom_call" | custom-call | flops 12000000000 | bytes 1048576 | tf_op jit(solution)/shard_map/weight_grads/pallas_call | solution.py:255
  158.7 2.8 %merge.3 = (bf16[1440,128]{1,0:T(8,128)(2,1)}, bf16[4,128]{1,0:T(4,128)(2,1)}) custom-call(bf16[192,128]{1,0:T(8,128)(2,1)} %get-tuple-element.110.hot_ref, bf16[8,2,24,1444]{3,2,1,0:T(8,128)(2,1)} %all-to-all-done.4.back_ref, bf16[128,1444]{1,0:T(8,128)(2,1)} %collective-permute-done.12.refs_0_, bf16[128,1444]{1,0:T(8,128)(2,1)} %copy-done, ...), custom_call_target="tpu_custom_call" | custom-call | flops 1048576 | bytes 65536 | tf_op jit(solution)/shard_map/merge/pallas_call | solution.py:206
  (46 shorter events, 0.1 us)
Async XLA Ops:
  4.0 10.8 %collective-permute-start.1 = (bf16[2896,128]{1,0:T(8,128)(2,1)}, bf16[2896,128]{1,0:T(8,128)(2,1)S(1)}, u32[]{:S(2)}, u32[]{:S(2)}) collective-permute-start(bf16[2896,128]{1,0:T(8,128)(2,1)} %get-tuple-element.111), channel_id=1, source_target_pairs={{1,2},{2,1},{5,6},{6,5},{9,10},{10,9},{13,14},{14,13},{17,18},{18,... | collective-permute-start | bytes 2224136 | tf_op jit(solution)/shard_map/ppermute | solution.py:281
  4.7 21.0 %collective-permute-start = (bf16[2896,128]{1,0:T(8,128)(2,1)}, bf16[2896,128]{1,0:T(8,128)(2,1)}, u32[]{:S(2)}, u32[]{:S(2)}) collective-permute-start(bf16[2896,128]{1,0:T(8,128)(2,1)} %get-tuple-element.111), channel_id=1, source_target_pairs={{0,1},{1,0},{2,3},{3,2},{4,5},{5,4},{6,7},{7,6},{8,9},{9,8},{10,11... | collective-permute-start | bytes 2224136 | tf_op jit(solution)/shard_map/ppermute | solution.py:281
  9.4 21.9 %all-to-all-start = ((bf16[8,24,2976]{2,1,0:T(8,128)(2,1)}), bf16[8,24,2976]{2,1,0:T(8,128)(2,1)}, u32[]{:S(2)}, u32[]{:S(2)}) async-start(bf16[8,24,2976]{2,1,0:T(8,128)(2,1)} %get-tuple-element.114), calls=%async_computation | async-start | bytes 2359296 | tf_op jit(solution)/shard_map/all_to_all | solution.py:284
  14.8 16.5 %copy-start.11 = (bf16[2896,128]{1,0:T(8,128)(2,1)}, bf16[2896,128]{1,0:T(8,128)(2,1)S(1)}, u32[]{:S(2)}) copy-start(bf16[2896,128]{1,0:T(8,128)(2,1)S(1)} %collective-permute-done.1.refs_0_) | copy-start | bytes 2224132
  25.7 22.7 %collective-permute-start.2 = (bf16[2896,128]{1,0:T(8,128)(2,1)}, bf16[2896,128]{1,0:T(8,128)(2,1)}, u32[]{:S(2)}, u32[]{:S(2)}) collective-permute-start(bf16[2896,128]{1,0:T(8,128)(2,1)} %collective-permute-done.refs_0_), channel_id=1, source_target_pairs={{1,2},{2,1},{5,6},{6,5},{9,10},{10,9},{13,14},{14,13},{17,18},{18,... | collective-permute-start | bytes 2224136 | tf_op jit(solution)/shard_map/ppermute | solution.py:281
  27.3 21.1 %collective-permute-start.3 = (bf16[2896,128]{1,0:T(8,128)(2,1)S(1)}, bf16[2896,128]{1,0:T(8,128)(2,1)}, u32[]{:S(2)}, u32[]{:S(2)}) collective-permute-start(bf16[2896,128]{1,0:T(8,128)(2,1)S(1)} %collective-permute-done.1.refs_0_), channel_id=1, source_target_pairs={{1,0},{2,3},{5,4},{6,7},{9,8},{10,11},{13,12},{14,15},{17,16},{18,... | collective-permute-start | bytes 2224136 | tf_op jit(solution)/shard_map/ppermute | solution.py:281
  31.3 21.4 %all-to-all-start.1 = ((bf16[8,24,2976]{2,1,0:T(8,128)(2,1)}), bf16[8,24,2976]{2,1,0:T(8,128)(2,1)}, u32[]{:S(2)}, u32[]{:S(2)}) async-start(bf16[8,24,2976]{2,1,0:T(8,128)(2,1)} %get-tuple-element.121), calls=%async_computation.1 | async-start | bytes 2359296 | tf_op jit(solution)/shard_map/all_to_all | solution.py:284
  48.4 21.6 %collective-permute-start.4 = (bf16[2896,128]{1,0:T(8,128)(2,1)}, bf16[2896,128]{1,0:T(8,128)(2,1)S(1)}, u32[]{:S(2)}, u32[]{:S(2)}) collective-permute-start(bf16[2896,128]{1,0:T(8,128)(2,1)} %collective-permute-done.2.refs_0_), channel_id=1, source_target_pairs={{1,0},{2,3},{5,4},{6,7},{9,8},{10,11},{13,12},{14,15},{17,16},{18,... | collective-permute-start | bytes 2224136 | tf_op jit(solution)/shard_map/ppermute | solution.py:281
  52.7 21.2 %all-to-all-start.2 = ((bf16[8,24,2976]{2,1,0:T(8,128)(2,1)}), bf16[8,24,2976]{2,1,0:T(8,128)(2,1)}, u32[]{:S(2)}, u32[]{:S(2)}) async-start(bf16[8,24,2976]{2,1,0:T(8,128)(2,1)} %get-tuple-element.127), calls=%async_computation.2 | async-start | bytes 2359296 | tf_op jit(solution)/shard_map/all_to_all | solution.py:284
  70.0 0.9 copy-start.12
  73.9 28.6 %all-to-all-start.3 = ((bf16[8,24,2976]{2,1,0:T(8,128)(2,1)}), bf16[8,24,2976]{2,1,0:T(8,128)(2,1)}, u32[]{:S(2)}, u32[]{:S(2)}) async-start(bf16[8,24,2976]{2,1,0:T(8,128)(2,1)} %get-tuple-element.137), calls=%async_computation.3 | async-start | bytes 2359296 | tf_op jit(solution)/shard_map/all_to_all | solution.py:284
  90.7 3.9 %collective-permute-start.5 = (bf16[24,1444]{1,0:T(8,128)(2,1)}, bf16[24,1444]{1,0:T(8,128)(2,1)S(1)}, u32[]{:S(2)}, u32[]{:S(2)}) collective-permute-start(bf16[24,1444]{1,0:T(8,128)(2,1)} %get-tuple-element.144), channel_id=1, source_target_pairs={{0,4},{4,0},{8,12},{12,8},{16,20},{20,16},{24,28},{28,24},{1,5},{5... | collective-permute-start | bytes 207944 | tf_op jit(solution)/shard_map/ppermute | solution.py:296
  90.9 6.0 %collective-permute-start.6 = (bf16[24,1444]{1,0:T(8,128)(2,1)}, bf16[24,1444]{1,0:T(8,128)(2,1)S(1)}, u32[]{:S(2)}, u32[]{:S(2)}) collective-permute-start(bf16[24,1444]{1,0:T(8,128)(2,1)} %get-tuple-element.145), channel_id=1, source_target_pairs={{0,8},{4,12},{8,0},{12,4},{16,24},{20,28},{24,16},{28,20},{1,9},{5... | collective-permute-start | bytes 207944 | tf_op jit(solution)/shard_map/ppermute | solution.py:296
  92.6 6.3 %collective-permute-start.7 = (bf16[24,1444]{1,0:T(8,128)(2,1)}, bf16[24,1444]{1,0:T(8,128)(2,1)S(1)}, u32[]{:S(2)}, u32[]{:S(2)}) collective-permute-start(bf16[24,1444]{1,0:T(8,128)(2,1)} %get-tuple-element.146), channel_id=1, source_target_pairs={{0,12},{4,8},{8,4},{12,0},{16,28},{20,24},{24,20},{28,16},{1,13},{... | collective-permute-start | bytes 207944 | tf_op jit(solution)/shard_map/ppermute | solution.py:296
  93.0 5.9 %collective-permute-start.8 = (bf16[24,1444]{1,0:T(8,128)(2,1)}, bf16[24,1444]{1,0:T(8,128)(2,1)S(1)}, u32[]{:S(2)}, u32[]{:S(2)}) collective-permute-start(bf16[24,1444]{1,0:T(8,128)(2,1)} %get-tuple-element.147), channel_id=1, source_target_pairs={{0,16},{4,20},{8,24},{12,28},{16,0},{20,4},{24,8},{28,12},{1,17},{... | collective-permute-start | bytes 207944 | tf_op jit(solution)/shard_map/ppermute | solution.py:296
  94.4 6.1 %collective-permute-start.9 = (bf16[24,1444]{1,0:T(8,128)(2,1)}, bf16[24,1444]{1,0:T(8,128)(2,1)S(1)}, u32[]{:S(2)}, u32[]{:S(2)}) collective-permute-start(bf16[24,1444]{1,0:T(8,128)(2,1)} %get-tuple-element.148), channel_id=1, source_target_pairs={{0,20},{4,16},{8,28},{12,24},{16,4},{20,0},{24,12},{28,8},{1,21},{... | collective-permute-start | bytes 207944 | tf_op jit(solution)/shard_map/ppermute | solution.py:296
  94.6 7.8 %copy-start.4 = (bf16[24,1444]{1,0:T(8,128)(2,1)}, bf16[24,1444]{1,0:T(8,128)(2,1)S(1)}, u32[]{:S(2)}) copy-start(bf16[24,1444]{1,0:T(8,128)(2,1)S(1)} %collective-permute-done.5.refs_1_) | copy-start | bytes 207940
  94.6 5.8 %collective-permute-start.10 = (bf16[24,1444]{1,0:T(8,128)(2,1)}, bf16[24,1444]{1,0:T(8,128)(2,1)S(1)}, u32[]{:S(2)}, u32[]{:S(2)}) collective-permute-start(bf16[24,1444]{1,0:T(8,128)(2,1)} %get-tuple-element.149), channel_id=1, source_target_pairs={{0,24},{4,28},{8,16},{12,20},{16,8},{20,12},{24,0},{28,4},{1,25},{... | collective-permute-start | bytes 207944 | tf_op jit(solution)/shard_map/ppermute | solution.py:296
  97.0 5.5 %copy-start.5 = (bf16[24,1444]{1,0:T(8,128)(2,1)}, bf16[24,1444]{1,0:T(8,128)(2,1)S(1)}, u32[]{:S(2)}) copy-start(bf16[24,1444]{1,0:T(8,128)(2,1)S(1)} %collective-permute-done.6.refs_2_) | copy-start | bytes 207940
  97.0 5.5 %collective-permute-start.11 = (bf16[24,1444]{1,0:T(8,128)(2,1)}, bf16[24,1444]{1,0:T(8,128)(2,1)S(1)}, u32[]{:S(2)}, u32[]{:S(2)}) collective-permute-start(bf16[24,1444]{1,0:T(8,128)(2,1)} %get-tuple-element.150), channel_id=1, source_target_pairs={{0,28},{4,24},{8,20},{12,16},{16,12},{20,8},{24,4},{28,0},{1,29},{... | collective-permute-start | bytes 207944 | tf_op jit(solution)/shard_map/ppermute | solution.py:296
  98.8 3.7 %copy-start.6 = (bf16[24,1444]{1,0:T(8,128)(2,1)}, bf16[24,1444]{1,0:T(8,128)(2,1)S(1)}, u32[]{:S(2)}) copy-start(bf16[24,1444]{1,0:T(8,128)(2,1)S(1)} %collective-permute-done.7.refs_3_) | copy-start | bytes 207940
  98.8 3.7 %copy-start.7 = (bf16[24,1444]{1,0:T(8,128)(2,1)}, bf16[24,1444]{1,0:T(8,128)(2,1)S(1)}, u32[]{:S(2)}) copy-start(bf16[24,1444]{1,0:T(8,128)(2,1)S(1)} %collective-permute-done.8.refs_4_) | copy-start | bytes 207940
  100.4 2.1 %copy-start.8 = (bf16[24,1444]{1,0:T(8,128)(2,1)}, bf16[24,1444]{1,0:T(8,128)(2,1)S(1)}, u32[]{:S(2)}) copy-start(bf16[24,1444]{1,0:T(8,128)(2,1)S(1)} %collective-permute-done.9.refs_5_) | copy-start | bytes 207940
  100.4 2.1 %copy-start.9 = (bf16[24,1444]{1,0:T(8,128)(2,1)}, bf16[24,1444]{1,0:T(8,128)(2,1)S(1)}, u32[]{:S(2)}) copy-start(bf16[24,1444]{1,0:T(8,128)(2,1)S(1)} %collective-permute-done.10.refs_6_) | copy-start | bytes 207940
  102.5 0.6 copy-start.10
  105.4 4.7 %copy-start.1 = (bf16[128,1444]{1,0:T(8,128)(2,1)S(1)}, bf16[128,1444]{1,0:T(8,128)(2,1)}, u32[]{:S(2)}) copy-start(bf16[128,1444]{1,0:T(8,128)(2,1)} %gather.2) | copy-start | bytes 1108996
  105.4 29.5 %all-to-all-start.4 = ((bf16[8,2,24,1444]{3,2,1,0:T(8,128)(2,1)}), bf16[8,2,24,1444]{3,2,1,0:T(8,128)(2,1)}, u32[]{:S(2)}, u32[]{:S(2)}) async-start(bf16[8,2,24,1444]{3,2,1,0:T(8,128)(2,1)} %get-tuple-element.161), calls=%async_computation.4 | async-start | bytes 2359296 | tf_op jit(solution)/shard_map/all_to_all | solution.py:284
  110.0 31.2 %collective-permute-start.13 = (bf16[128,1444]{1,0:T(8,128)(2,1)S(1)}, bf16[128,1444]{1,0:T(8,128)(2,1)S(1)}, u32[]{:S(2)}, u32[]{:S(2)}) collective-permute-start(bf16[128,1444]{1,0:T(8,128)(2,1)S(1)} %copy-done.1), channel_id=1, source_target_pairs={{0,2},{1,3},{2,0},{3,1},{4,6},{5,7},{6,4},{7,5},{8,10},{9,11},{10,... | collective-permute-start | bytes 1109000 | tf_op jit(solution)/shard_map/ppermute | solution.py:281
  125.8 3.8 %collective-permute-start.14 = (bf16[24,1444]{1,0:T(8,128)(2,1)}, bf16[24,1444]{1,0:T(8,128)(2,1)S(1)}, u32[]{:S(2)}, u32[]{:S(2)}) collective-permute-start(bf16[24,1444]{1,0:T(8,128)(2,1)} %get-tuple-element.171), channel_id=1, source_target_pairs={{0,4},{4,0},{8,12},{12,8},{16,20},{20,16},{24,28},{28,24},{1,5},{5... | collective-permute-start | bytes 207944 | tf_op jit(solution)/shard_map/ppermute | solution.py:296
  126.6 4.1 %collective-permute-start.15 = (bf16[24,1444]{1,0:T(8,128)(2,1)}, bf16[24,1444]{1,0:T(8,128)(2,1)S(1)}, u32[]{:S(2)}, u32[]{:S(2)}) collective-permute-start(bf16[24,1444]{1,0:T(8,128)(2,1)} %get-tuple-element.172), channel_id=1, source_target_pairs={{0,8},{4,12},{8,0},{12,4},{16,24},{20,28},{24,16},{28,20},{1,9},{5... | collective-permute-start | bytes 207944 | tf_op jit(solution)/shard_map/ppermute | solution.py:296
  127.9 5.0 %collective-permute-start.16 = (bf16[24,1444]{1,0:T(8,128)(2,1)}, bf16[24,1444]{1,0:T(8,128)(2,1)}, u32[]{:S(2)}, u32[]{:S(2)}) collective-permute-start(bf16[24,1444]{1,0:T(8,128)(2,1)} %get-tuple-element.173), channel_id=1, source_target_pairs={{0,12},{4,8},{8,4},{12,0},{16,28},{20,24},{24,20},{28,16},{1,13},{... | collective-permute-start | bytes 207944 | tf_op jit(solution)/shard_map/ppermute | solution.py:296
  128.3 8.9 %collective-permute-start.17 = (bf16[24,1444]{1,0:T(8,128)(2,1)}, bf16[24,1444]{1,0:T(8,128)(2,1)}, u32[]{:S(2)}, u32[]{:S(2)}) collective-permute-start(bf16[24,1444]{1,0:T(8,128)(2,1)} %get-tuple-element.174), channel_id=1, source_target_pairs={{0,16},{4,20},{8,24},{12,28},{16,0},{20,4},{24,8},{28,12},{1,17},{... | collective-permute-start | bytes 207944 | tf_op jit(solution)/shard_map/ppermute | solution.py:296
  129.6 8.3 %copy-start.2 = (bf16[24,1444]{1,0:T(8,128)(2,1)}, bf16[24,1444]{1,0:T(8,128)(2,1)S(1)}, u32[]{:S(2)}) copy-start(bf16[24,1444]{1,0:T(8,128)(2,1)S(1)} %collective-permute-done.14.refs_1_) | copy-start | bytes 207940
  129.6 7.6 %collective-permute-start.18 = (bf16[24,1444]{1,0:T(8,128)(2,1)}, bf16[24,1444]{1,0:T(8,128)(2,1)}, u32[]{:S(2)}, u32[]{:S(2)}) collective-permute-start(bf16[24,1444]{1,0:T(8,128)(2,1)} %get-tuple-element.175), channel_id=1, source_target_pairs={{0,20},{4,16},{8,28},{12,24},{16,4},{20,0},{24,12},{28,8},{1,21},{... | collective-permute-start | bytes 207944 | tf_op jit(solution)/shard_map/ppermute | solution.py:296
  130.6 7.3 %copy-start.3 = (bf16[24,1444]{1,0:T(8,128)(2,1)}, bf16[24,1444]{1,0:T(8,128)(2,1)S(1)}, u32[]{:S(2)}) copy-start(bf16[24,1444]{1,0:T(8,128)(2,1)S(1)} %collective-permute-done.15.refs_2_) | copy-start | bytes 207940
  130.6 6.6 %collective-permute-start.19 = (bf16[24,1444]{1,0:T(8,128)(2,1)}, bf16[24,1444]{1,0:T(8,128)(2,1)}, u32[]{:S(2)}, u32[]{:S(2)}) collective-permute-start(bf16[24,1444]{1,0:T(8,128)(2,1)} %get-tuple-element.176), channel_id=1, source_target_pairs={{0,24},{4,28},{8,16},{12,20},{16,8},{20,12},{24,0},{28,4},{1,25},{... | collective-permute-start | bytes 207944 | tf_op jit(solution)/shard_map/ppermute | solution.py:296
  132.9 5.0 %collective-permute-start.20 = (bf16[24,1444]{1,0:T(8,128)(2,1)}, bf16[24,1444]{1,0:T(8,128)(2,1)}, u32[]{:S(2)}, u32[]{:S(2)}) collective-permute-start(bf16[24,1444]{1,0:T(8,128)(2,1)} %get-tuple-element.177), channel_id=1, source_target_pairs={{0,28},{4,24},{8,20},{12,16},{16,12},{20,8},{24,4},{28,0},{1,29},{... | collective-permute-start | bytes 207944 | tf_op jit(solution)/shard_map/ppermute | solution.py:296
  137.2 21.4 %collective-permute-start.12 = (bf16[128,1444]{1,0:T(8,128)(2,1)}, bf16[128,1444]{1,0:T(8,128)(2,1)}, u32[]{:S(2)}, u32[]{:S(2)}) collective-permute-start(bf16[128,1444]{1,0:T(8,128)(2,1)} %merge.2), channel_id=1, source_target_pairs={{0,1},{1,0},{2,3},{3,2},{4,5},{5,4},{6,7},{7,6},{8,9},{9,8},{10,11... | collective-permute-start | bytes 1109000 | tf_op jit(solution)/shard_map/ppermute | solution.py:281
  140.1 18.5 %collective-permute-start.21 = (bf16[128,1444]{1,0:T(8,128)(2,1)}, bf16[128,1444]{1,0:T(8,128)(2,1)}, u32[]{:S(2)}, u32[]{:S(2)}) collective-permute-start(bf16[128,1444]{1,0:T(8,128)(2,1)} %gather.3), channel_id=1, source_target_pairs={{0,3},{1,2},{2,1},{3,0},{4,7},{5,6},{6,5},{7,4},{8,11},{9,10},{10,... | collective-permute-start | bytes 1109000 | tf_op jit(solution)/shard_map/ppermute | solution.py:281
  141.2 17.4 %copy-start = (bf16[128,1444]{1,0:T(8,128)(2,1)}, bf16[128,1444]{1,0:T(8,128)(2,1)S(1)}, u32[]{:S(2)}) copy-start(bf16[128,1444]{1,0:T(8,128)(2,1)S(1)} %collective-permute-done.13.refs_1_) | copy-start | bytes 1108996

commit v2 on v1

--- a/solution.py
+++ b/solution.py
@@ -136,10 +136,13 @@
         back_ref[:, cut] = dot(dh, wg[cut, :], 1, 1) + dot(du, wu[cut, :], 1, 1)
     back_ref[:, width:] = jnp.where(mine, gp, 0.0)
     if fan:
-        for j, ret_ref in enumerate(ahead):
-            cap = ret_ref.shape[0]
-            at = pl.multiple_of((place_ref[0] ^ j) * cap, 8)
-            ret_ref[...] = back_ref[pl.ds(at, cap), :].astype(BF)
+        prev, rets = (ahead[0], ahead[1:]) if ahead[-1].shape[0] > 1 else (None, ahead)
+        for j, ret_ref in enumerate(rets):
+            depth, cap, _ = ret_ref.shape
+            island = place_ref[0] ^ j
+            if prev is not None:
+                ret_ref[:depth - 1] = prev[island]
+            ret_ref[depth - 1] = back_ref[pl.ds(pl.multiple_of(island * cap, 8), cap), :].astype(BF)
         return
     ret_ref = ahead[-1]
     islands, depth, cap, cols = ret_ref.shape
@@ -154,7 +157,7 @@
     cols = (width, hidden, hidden, hidden)
     before = [] if prev is None else [prev]
     shape = (rows // islands, width + topk)
-    back = [shape] * islands if fan else [(islands, depth) + shape]
+    back = [(depth,) + shape] * islands if fan else [(islands, depth) + shape]
     outs = pl.pallas_call(
         functools.partial(expert_kernel, width, hidden, lane, topk, n, 512, fan),
         out_shape=[jax.ShapeDtypeStruct(o, BF) for o in back + [(rows, c) for c in cols]],
@@ -181,19 +184,19 @@
     refs[-1][...] = total[:, cols - topk:].T.astype(BF)
 
 
-def gather_kernel(place_ref, hot_ref, *refs):
+def gather_kernel(at, place_ref, hot_ref, *refs):
     backs, out_ref, rows_ref = refs[:-2], refs[-2], refs[-1]
     for j, back in enumerate(backs):
-        cap = back.shape[0]
-        at = pl.multiple_of((place_ref[0] ^ j) * cap, 8)
-        rows_ref[pl.ds(at, cap), :] = back[...].astype(F32)
+        cap = back.shape[1]
+        row = pl.multiple_of((place_ref[0] ^ j) * cap, 8)
+        rows_ref[pl.ds(row, cap), :] = back[at].astype(F32)
     out_ref[...] = dot(hot_ref[...], rows_ref[...].astype(BF), 0, 0).astype(BF)
 
 
-def gather(place, hot, backs):
-    cols = backs[0].shape[1]
+def gather(place, hot, backs, at):
+    cols = backs[0].shape[2]
     return pl.pallas_call(
-        gather_kernel, out_shape=jax.ShapeDtypeStruct((hot.shape[1], cols), BF),
+        functools.partial(gather_kernel, at), out_shape=jax.ShapeDtypeStruct((hot.shape[1], cols), BF),
         in_specs=[SMEM] + [VMEM] * (1 + len(backs)), out_specs=VMEM,
         scratch_shapes=[pltpu.VMEM((hot.shape[0], cols), F32)],
         compiler_params=GRANT, cost_estimate=COST, name="gather",
@@ -313,31 +316,31 @@
     rows2, hot2 = take(two_in, two_out)
     got1, rows2, keep0 = seal((got1, rows2, keep0))
     got2 = deal(rows2)
-    ret01, keep1 = work(got1, ret0)
-    three, ret01 = seal((three, ret01))
+    ret1, keep1 = work(got1)
+    three, ret1 = seal((three, ret1))
     rows3, hot3 = take(near, three)
     got2, rows3, keep1 = seal((got2, rows3, keep1))
     got3 = deal(rows3)
-    ret2, keep2 = work(got2, fan=True)
-    back2 = give(ret2)
-    got3, keep2, back2 = seal((got3, keep2, back2))
-    merge2 = gather(place, hot2, back2)
+    ret12, keep2 = work(got2, ret1, True)
+    back12 = give(ret12)
+    got3, keep2 = seal((got3, keep2))
+    ret3, keep3 = work(got3, fan=True)
+    ret3, keep3, back12 = seal((ret3, keep3, back12))
+    merge2 = gather(place, hot2, back12, 1)
     part2 = part(merge2, 2)
-    merge2, ret01, got3 = seal((merge2, ret01, got3))
-    back01 = a2a(ret01)
-    ret3, keep3 = work(got3, fan=True)
+    merge2, ret3 = seal((merge2, ret3))
     back3 = give(ret3)
-    back01, keep3 = seal((back01, keep3))
-    merge1 = merge(hot1, back01, 1, topk)
+    merge1 = gather(place, hot1, back12, 0)
     part1 = part(merge1, 1)
     merge1, back3 = seal((merge1, back3))
-    merge3 = gather(place, hot3, back3)
+    merge3 = gather(place, hot3, back3, 0)
     part3 = part(merge3, 3)
-    part2, merge3, keep3 = seal((part2, merge3, keep3))
+    part2, merge3, keep3, ret0 = seal((part2, merge3, keep3, ret0))
+    back0 = a2a(ret0)
     ys, a, dh, du = zip(keep0, keep1, keep2, keep3)
     gg, gu, gd = weight_grads((got0, got1, got2, got3), dh, du, a, ys)
     part1, part2, gg = seal((part1, part2, gg))
-    grad_in, grad_probs = merge(hot0, back01, 0, topk, (part1, part2, part3))
+    grad_in, grad_probs = merge(hot0, back0, 0, topk, (part1, part2, part3))
     return grad_in.T, grad_probs.T, gg, gu, gd
 
 

time: 164 us -> 163 us (level)
  starting transfers between devices: 57.8 us -> 56.1 us
    pallas_call x2 -> x3, Pallas kernels: 4.51 us -> 7.15 us  [gather(): pl.pallas_call(functools.partial(gather_kernel, at), out_shape=jax.ShapeD...]
    pallas_call x2 -> x1, Pallas kernels: 5.18 us -> 2.63 us  [merge(): pl.pallas_call(functools.partial(merge_kernel, topk, at), out_shape=[jax....]
    ppermute x8, waiting for transfers between devices: 11.2 us -> 13 us  [send(): return lax.ppermute(v, 'local', pairs)]
    ppermute x14, waiting for transfers between devices: 4.82 us -> 3.14 us  [give(): lax.ppermute(rets[j], 'island', [(i, i ^ j) for i in range(islands)])]
where the time goes in v2:
time: 163 us; the launch traced here: 162 us
  Pallas kernels  84.9 us (52%)
  starting transfers between devices  56.1 us (34%)
  waiting for transfers between devices  16.2 us (10%)
  local copies, waits for them, and re-layouts  3.06 us (2%)
    pallas_call x4, Pallas kernels, expert(): pl.pallas_call(functools.partial(expert_kernel, width, hidden, lane, topk...  46.4 us
    all_to_all x5, starting transfers between devices, a2a(): return lax.all_to_all(v, 'island', 0, 0, tiled=True)  25.3 us
    pallas_call x1, Pallas kernels, weight_grads(): pl.pallas_call(functools.partial(weights_kernel, [len(v) for v in (x, dh,...  17.3 us
    ppermute x14, starting transfers between devices, give(): lax.ppermute(rets[j], 'island', [(i, i ^ j) for i in range(islands)])  15.9 us
    ppermute x8, starting transfers between devices, send(): return lax.ppermute(v, 'local', pairs)  14.9 us
    ppermute x8, waiting for transfers between devices, send(): return lax.ppermute(v, 'local', pairs)  13 us
    pallas_call x3, Pallas kernels, pick(): pl.pallas_call(functools.partial(pick_kernel, width, meta, lane, islands,...  8.71 us
    pallas_call x3, Pallas kernels, gather(): pl.pallas_call(functools.partial(gather_kernel, at), out_shape=jax.ShapeD...  7.15 us
  transfers between devices with their start and end apart: 27, of which 6 were waited for; matrix products, arithmetic and copies ran while one was open for 0% of the time, Pallas kernels for 48%

profile of v2, /device:TPU:1, one launch (start us, length us, event | category | flops | bytes accessed | tf_op | source)
XLA Modules:
  0.0 161.9 jit_solution(16873502982092675968)
XLA Ops:
  0.6 0.7 pad_add_fusion.place_ref
  1.3 2.8 %pack.1 = (bf16[2896,128]{1,0:T(8,128)(2,1)}, bf16[8,24,2976]{2,1,0:T(8,128)(2,1)}, bf16[192,128]{1,0:T(8,128)(2,1)}) custom-call(s32[3]{0:T(128)} %pad_add_fusion.place_ref, bf16[1440,128]{1,0:T(8,128)(2,1)} %bitcast.28, bf16[4,128]{1,0:T(4,128)(2,1)} %bitcast.31, s32[4,128]{1,0:T(4,128)} %bitcast.30, bf16[1440,128]{1,0:T(8,128)(2,1)} %bitcast.29), custom_call_target="tpu_custom_call" | custom-call | flops 1048576 | bytes 65536 | tf_op jit(solution)/shard_map/pack/pallas_call | solution.py:231
  4.1 0.7 collective-permute-start.1
  4.8 4.7 %collective-permute-start = (bf16[2896,128]{1,0:T(8,128)(2,1)}, bf16[2896,128]{1,0:T(8,128)(2,1)}, u32[]{:S(2)}, u32[]{:S(2)}) collective-permute-start(bf16[2896,128]{1,0:T(8,128)(2,1)} %get-tuple-element.125), channel_id=1, source_target_pairs={{0,1},{1,0},{2,3},{3,2},{4,5},{5,4},{6,7},{7,6},{8,9},{9,8},{10,11... | collective-permute-start | bytes 2224136 | tf_op jit(solution)/shard_map/ppermute | solution.py:284
  9.5 5.4 %all-to-all-start = ((bf16[8,24,2976]{2,1,0:T(8,128)(2,1)}), bf16[8,24,2976]{2,1,0:T(8,128)(2,1)}, u32[]{:S(2)}, u32[]{:S(2)}) async-start(bf16[8,24,2976]{2,1,0:T(8,128)(2,1)} %get-tuple-element.128), calls=%async_computation | async-start | bytes 2359296 | tf_op jit(solution)/shard_map/all_to_all | solution.py:287
  14.8 10.9 %collective-permute-done.refs_0_ = bf16[2896,128]{1,0:T(8,128)(2,1)} collective-permute-done((bf16[2896,128]{1,0:T(8,128)(2,1)}, bf16[2896,128]{1,0:T(8,128)(2,1)}, u32[]{:S(2)}, u32[]{:S(2)}) %collective-permute-start) | collective-permute-done | bytes 741408 | tf_op jit(solution)/shard_map/ppermute | solution.py:284
  25.8 1.5 collective-permute-start.2
  27.3 1.3 collective-permute-start.3
  28.6 2.8 %pick.3 = (bf16[8,24,2976]{2,1,0:T(8,128)(2,1)}, bf16[192,128]{1,0:T(8,128)(2,1)}) custom-call(s32[3]{0:T(128)} %pad_add_fusion.place_ref, bf16[2896,128]{1,0:T(8,128)(2,1)} %collective-permute-done.refs_0_), custom_call_target="tpu_custom_call" | custom-call | flops 12000000000 | bytes 1048576 | tf_op jit(solution)/shard_map/pick/pallas_call | solution.py:88
  31.3 5.7 %all-to-all-start.1 = ((bf16[8,24,2976]{2,1,0:T(8,128)(2,1)}), bf16[8,24,2976]{2,1,0:T(8,128)(2,1)}, u32[]{:S(2)}, u32[]{:S(2)}) async-start(bf16[8,24,2976]{2,1,0:T(8,128)(2,1)} %get-tuple-element.135), calls=%async_computation.1 | async-start | bytes 2359296 | tf_op jit(solution)/shard_map/all_to_all | solution.py:287
  37.0 11.4 %expert.4 = (bf16[8,1,24,1444]{3,2,1,0:T(8,128)(2,1)}, bf16[192,1440]{1,0:T(8,128)(2,1)}, bf16[192,1440]{1,0:T(8,128)(2,1)}, bf16[192,1440]{1,0:T(8,128)(2,1)}, bf16[192,1440]{1,0:T(8,128)(2,1)}) custom-call(s32[3]{0:T(128)} %pad_add_fusion.place_ref, bf16[192,2976]{1,0:T(8,128)(2,1)} %bitcast.7.got_ref.refs_0_, bf16[1440,1440]{1,0:T(8,128)(2,1)} %bitcast.16, ...), custom_call_target="tpu_custom_call" | custom-call | flops 1048576 | bytes 65536 | tf_op jit(solution)/shard_map/expert/pallas_call | solution.py:161
  48.4 1.3 collective-permute-start.4
  49.7 3.0 %pick.4 = (bf16[8,24,2976]{2,1,0:T(8,128)(2,1)}, bf16[192,128]{1,0:T(8,128)(2,1)}) custom-call(s32[3]{0:T(128)} %pad_add_fusion.place_ref, bf16[2896,128]{1,0:T(8,128)(2,1)} %collective-permute-done.2.refs_0_, bf16[2896,128]{1,0:T(8,128)(2,1)} %collective-permute-done.3.refs_1_), custom_call_target="tpu_custom_call" | custom-call | flops 12000000000 | bytes 1048576 | tf_op jit(solution)/shard_map/pick/pallas_call | solution.py:88
  52.7 5.4 %all-to-all-start.2 = ((bf16[8,24,2976]{2,1,0:T(8,128)(2,1)}), bf16[8,24,2976]{2,1,0:T(8,128)(2,1)}, u32[]{:S(2)}, u32[]{:S(2)}) async-start(bf16[8,24,2976]{2,1,0:T(8,128)(2,1)} %get-tuple-element.141), calls=%async_computation.2 | async-start | bytes 2359296 | tf_op jit(solution)/shard_map/all_to_all | solution.py:287
  58.1 11.4 %expert.5 = (bf16[8,1,24,1444]{3,2,1,0:T(8,128)(2,1)}, bf16[192,1440]{1,0:T(8,128)(2,1)}, bf16[192,1440]{1,0:T(8,128)(2,1)}, bf16[192,1440]{1,0:T(8,128)(2,1)}, bf16[192,1440]{1,0:T(8,128)(2,1)}) custom-call(s32[3]{0:T(128)} %pad_add_fusion.place_ref, bf16[192,2976]{1,0:T(8,128)(2,1)} %bitcast.11.got_ref.refs_1_, bf16[1440,1440]{1,0:T(8,128)(2,1)} %bitcast.17, ...), custom_call_target="tpu_custom_call" | custom-call | flops 1048576 | bytes 65536 | tf_op jit(solution)/shard_map/expert/pallas_call | solution.py:161
  69.5 0.6 collective-permute-done.4.refs_1_
  70.1 0.9 copy-done.16
  70.9 3.0 %pick.5 = (bf16[8,24,2976]{2,1,0:T(8,128)(2,1)}, bf16[192,128]{1,0:T(8,128)(2,1)}) custom-call(s32[3]{0:T(128)} %pad_add_fusion.place_ref, bf16[2896,128]{1,0:T(8,128)(2,1)} %copy-done.15, bf16[2896,128]{1,0:T(8,128)(2,1)} %copy-done.16), custom_call_target="tpu_custom_call" | custom-call | flops 12000000000 | bytes 1048576 | tf_op jit(solution)/shard_map/pick/pallas_call | solution.py:88
  73.9 5.3 %all-to-all-start.3 = ((bf16[8,24,2976]{2,1,0:T(8,128)(2,1)}), bf16[8,24,2976]{2,1,0:T(8,128)(2,1)}, u32[]{:S(2)}, u32[]{:S(2)}) async-start(bf16[8,24,2976]{2,1,0:T(8,128)(2,1)} %get-tuple-element.150), calls=%async_computation.3 | async-start | bytes 2359296 | tf_op jit(solution)/shard_map/all_to_all | solution.py:287
  79.2 12.1 %expert.6 = (bf16[2,24,1444]{2,1,0:T(8,128)(2,1)}, bf16[2,24,1444]{2,1,0:T(8,128)(2,1)}, bf16[2,24,1444]{2,1,0:T(8,128)(2,1)}, bf16[2,24,1444]{2,1,0:T(8,128)(2,...) custom-call(s32[3]{0:T(128)} %pad_add_fusion.place_ref, ...), custom_call_target="tpu_custom_call" | custom-call | flops 1048576 | bytes 65536 | tf_op jit(solution)/shard_map/expert/pallas_call | solution.py:161
  91.3 0.4 collective-permute-start.5
  91.7 1.4 collective-permute-start.6
  93.1 0.4 collective-permute-start.7
  93.5 1.4 collective-permute-start.8
  94.9 0.3 collective-permute-start.9
  95.2 2.3 %collective-permute-start.10 = (bf16[2,24,1444]{2,1,0:T(8,128)(2,1)}, bf16[2,24,1444]{2,1,0:T(8,128)(2,1)S(1)}, u32[]{:S(2)}, u32[]{:S(2)}) collective-permute-start(bf16[2,24,1444]{2,1,0:T(8,128)(2,1)} %get-tuple-element.176), channel_id=1, source_target_pairs={{0,24},{4,28},{8,16},{12,20},{16,8},{20,12},{24,0},{28,4},{1,25},{... | collective-permute-start | bytes 415880 | tf_op jit(solution)/shard_map/ppermute | solution.py:299
  97.5 3.4 %collective-permute-start.11 = (bf16[2,24,1444]{2,1,0:T(8,128)(2,1)}, bf16[2,24,1444]{2,1,0:T(8,128)(2,1)}, u32[]{:S(2)}, u32[]{:S(2)}) collective-permute-start(bf16[2,24,1444]{2,1,0:T(8,128)(2,1)} %get-tuple-element.177), channel_id=1, source_target_pairs={{0,28},{4,24},{8,20},{12,16},{16,12},{20,8},{24,4},{28,0},{1,29},{... | collective-permute-start | bytes 415880 | tf_op jit(solution)/shard_map/ppermute | solution.py:299
  100.9 11.6 %expert.7 = (bf16[1,24,1444]{2,1,0:T(8,128)(2,1)}, bf16[1,24,1444]{2,1,0:T(8,128)(2,1)}, bf16[1,24,1444]{2,1,0:T(8,128)(2,1)}, bf16[1,24,1444]{2,1,0:T(8,128)(2,...) custom-call(s32[3]{0:T(128)} %pad_add_fusion.place_ref, ...), custom_call_target="tpu_custom_call" | custom-call | flops 1048576 | bytes 65536 | tf_op jit(solution)/shard_map/expert/pallas_call | solution.py:161
  112.6 0.6 copy-done.3
  113.3 2.4 %gather.3 = bf16[128,1444]{1,0:T(8,128)(2,1)} custom-call(s32[3]{0:T(128)} %pad_add_fusion.place_ref, bf16[192,128]{1,0:T(8,128)(2,1)} %get-tuple-element.134.hot_ref, bf16[2,24,1444]{2,1,0:T(8,128)(2,1)} %get-tuple-element.178.refs_0_, bf16[2,24,1444]{2,1,0:T(8,128)(2,1)} %copy-done.1, bf16[2,24,1444]{2,1,0:T(8,128)(2,1)} %copy-done.2, ...), custom_call_target="tpu_custom_call" | custom-call | flops 1048576 | bytes 65536 | tf_op jit(solution)/shard_map/gather/pallas_call | solution.py:198
  115.8 4.2 %collective-permute-start.12 = (bf16[128,1444]{1,0:T(8,128)(2,1)}, bf16[128,1444]{1,0:T(8,128)(2,1)S(1)}, u32[]{:S(2)}, u32[]{:S(2)}) collective-permute-start(bf16[128,1444]{1,0:T(8,128)(2,1)} %gather.3), channel_id=1, source_target_pairs={{0,2},{1,3},{2,0},{3,1},{4,6},{5,7},{6,4},{7,5},{8,10},{9,11},{10,... | collective-permute-start | bytes 1109000 | tf_op jit(solution)/shard_map/ppermute | solution.py:284
  120.0 0.3 collective-permute-start.14
  120.3 1.8 %collective-permute-start.15 = (bf16[1,24,1444]{2,1,0:T(8,128)(2,1)}, bf16[1,24,1444]{2,1,0:T(8,128)(2,1)S(1)}, u32[]{:S(2)}, u32[]{:S(2)}) collective-permute-start(bf16[1,24,1444]{2,1,0:T(8,128)(2,1)} %get-tuple-element.199), channel_id=1, source_target_pairs={{0,12},{4,8},{8,4},{12,0},{16,28},{20,24},{24,20},{28,16},{1,13},{... | collective-permute-start | bytes 207944 | tf_op jit(solution)/shard_map/ppermute | solution.py:299
  122.1 0.3 collective-permute-start.16
  122.4 1.1 collective-permute-start.17
  123.7 0.7 collective-permute-start.18
  124.4 1.9 %collective-permute-done.15.refs_3_ = bf16[1,24,1444]{2,1,0:T(8,128)(2,1)S(1)} collective-permute-done((bf16[1,24,1444]{2,1,0:T(8,128)(2,1)}, bf16[1,24,1444]{2,1,0:T(8,128)(2,1)S(1)}, u32[]{:S(2)}, u32[]{:S(2)}) %collective-permute-start.15) | collective-permute-done | bytes 69344 | tf_op jit(solution)/shard_map/ppermute | solution.py:299
  126.2 2.1 %collective-permute-start.19 = (bf16[1,24,1444]{2,1,0:T(8,128)(2,1)}, bf16[1,24,1444]{2,1,0:T(8,128)(2,1)S(1)}, u32[]{:S(2)}, u32[]{:S(2)}) collective-permute-start(bf16[1,24,1444]{2,1,0:T(8,128)(2,1)} %get-tuple-element.203), channel_id=1, source_target_pairs={{0,28},{4,24},{8,20},{12,16},{16,12},{20,8},{24,4},{28,0},{1,29},{... | collective-permute-start | bytes 207944 | tf_op jit(solution)/shard_map/ppermute | solution.py:299
  128.4 2.4 %gather.4 = bf16[128,1444]{1,0:T(8,128)(2,1)} custom-call(s32[3]{0:T(128)} %pad_add_fusion.place_ref, bf16[192,128]{1,0:T(8,128)(2,1)} %get-tuple-element.187.hot_ref, bf16[2,24,1444]{2,1,0:T(8,128)(2,1)} %get-tuple-element.178.refs_0_, bf16[2,24,1444]{2,1,0:T(8,128)(2,1)} %copy-done.1, bf16[2,24,1444]{2,1,0:T(8,128)(2,1)} %copy-done.2, ...), custom_call_target="tpu_custom_call" | custom-call | flops 1048576 | bytes 65536 | tf_op jit(solution)/shard_map/gather/pallas_call | solution.py:198
  131.0 1.0 collective-permute-done.19.refs_7_
  132.0 0.6 copy-done.14
  132.6 2.3 %gather.5 = bf16[128,1444]{1,0:T(8,128)(2,1)} custom-call(s32[3]{0:T(128)} %pad_add_fusion.place_ref, bf16[192,128]{1,0:T(8,128)(2,1)} %get-tuple-element.186.hot_ref, bf16[1,24,1444]{2,1,0:T(8,128)(2,1)} %get-tuple-element.204.refs_0_, bf16[1,24,1444]{2,1,0:T(8,128)(2,1)} %copy-done.8, bf16[1,24,1444]{2,1,0:T(8,128)(2,1)} %copy-done.9, ...), custom_call_target="tpu_custom_call" | custom-call | flops 1048576 | bytes 65536 | tf_op jit(solution)/shard_map/gather/pallas_call | solution.py:198
  134.9 1.1 collective-permute-start.21
  136.0 1.5 collective-permute-done.12.refs_1_
  137.6 3.5 %all-to-all-start.4 = ((bf16[8,1,24,1444]{3,2,1,0:T(8,128)(2,1)}), bf16[8,1,24,1444]{3,2,1,0:T(8,128)(2,1)S(1)}, u32[]{:S(2)}, u32[]{:S(2)}) async-start(bf16[8,1,24,1444]{3,2,1,0:T(8,128)(2,1)} %get-tuple-element.217), calls=%async_computation.4 | async-start | bytes 1179648 | tf_op jit(solution)/shard_map/all_to_all | solution.py:287
  141.1 17.3 %weight_grads.1 = (bf16[1,1440,1440]{2,1,0:T(8,128)(2,1)}, bf16[1,1440,1440]{2,1,0:T(8,128)(2,1)}, bf16[1,1440,1440]{2,1,0:T(8,128)(2,1)}) custom-call(bf16[192,2976]{1,0:T(8,128)(2,1)} %bitcast.7.got_ref.refs_0_, bf16[192,2976]{1,0:T(8,128)(2,1)} %bitcast.11.got_ref.refs_1_, bf16[192,2976]{1,0:T(8,128)(2,1)} %bitcast.12.got_ref.refs_2_, ...), custom_call_target="tpu_custom_call" | custom-call | flops 12000000000 | bytes 1048576 | tf_op jit(solution)/shard_map/weight_grads/pallas_call | solution.py:258
  158.4 0.8 copy-done
  159.2 2.6 %merge.1 = (bf16[1440,128]{1,0:T(8,128)(2,1)}, bf16[4,128]{1,0:T(4,128)(2,1)}) custom-call(bf16[192,128]{1,0:T(8,128)(2,1)} %get-tuple-element.124.hot_ref, bf16[8,1,24,1444]{3,2,1,0:T(8,128)(2,1)} %copy-done, bf16[128,1444]{1,0:T(8,128)(2,1)} %collective-permute-done.20.refs_0_, bf16[128,1444]{1,0:T(8,128)(2,1)} %copy-done.7, ...), custom_call_target="tpu_custom_call" | custom-call | flops 1048576 | bytes 65536 | tf_op jit(solution)/shard_map/merge/pallas_call | solution.py:209
  (54 shorter events, 0.5 us)
Async XLA Ops:
  4.1 10.8 %collective-permute-start.1 = (bf16[2896,128]{1,0:T(8,128)(2,1)}, bf16[2896,128]{1,0:T(8,128)(2,1)S(1)}, u32[]{:S(2)}, u32[]{:S(2)}) collective-permute-start(bf16[2896,128]{1,0:T(8,128)(2,1)} %get-tuple-element.125), channel_id=1, source_target_pairs={{1,2},{2,1},{5,6},{6,5},{9,10},{10,9},{13,14},{14,13},{17,18},{18,... | collective-permute-start | bytes 2224136 | tf_op jit(solution)/shard_map/ppermute | solution.py:284
  4.8 21.0 %collective-permute-start = (bf16[2896,128]{1,0:T(8,128)(2,1)}, bf16[2896,128]{1,0:T(8,128)(2,1)}, u32[]{:S(2)}, u32[]{:S(2)}) collective-permute-start(bf16[2896,128]{1,0:T(8,128)(2,1)} %get-tuple-element.125), channel_id=1, source_target_pairs={{0,1},{1,0},{2,3},{3,2},{4,5},{5,4},{6,7},{7,6},{8,9},{9,8},{10,11... | collective-permute-start | bytes 2224136 | tf_op jit(solution)/shard_map/ppermute | solution.py:284
  9.5 21.9 %all-to-all-start = ((bf16[8,24,2976]{2,1,0:T(8,128)(2,1)}), bf16[8,24,2976]{2,1,0:T(8,128)(2,1)}, u32[]{:S(2)}, u32[]{:S(2)}) async-start(bf16[8,24,2976]{2,1,0:T(8,128)(2,1)} %get-tuple-element.128), calls=%async_computation | async-start | bytes 2359296 | tf_op jit(solution)/shard_map/all_to_all | solution.py:287
  14.8 16.5 %copy-start.15 = (bf16[2896,128]{1,0:T(8,128)(2,1)}, bf16[2896,128]{1,0:T(8,128)(2,1)S(1)}, u32[]{:S(2)}) copy-start(bf16[2896,128]{1,0:T(8,128)(2,1)S(1)} %collective-permute-done.1.refs_0_) | copy-start | bytes 2224132
  25.8 22.6 %collective-permute-start.2 = (bf16[2896,128]{1,0:T(8,128)(2,1)}, bf16[2896,128]{1,0:T(8,128)(2,1)}, u32[]{:S(2)}, u32[]{:S(2)}) collective-permute-start(bf16[2896,128]{1,0:T(8,128)(2,1)} %collective-permute-done.refs_0_), channel_id=1, source_target_pairs={{1,2},{2,1},{5,6},{6,5},{9,10},{10,9},{13,14},{14,13},{17,18},{18,... | collective-permute-start | bytes 2224136 | tf_op jit(solution)/shard_map/ppermute | solution.py:284
  27.3 21.1 %collective-permute-start.3 = (bf16[2896,128]{1,0:T(8,128)(2,1)S(1)}, bf16[2896,128]{1,0:T(8,128)(2,1)}, u32[]{:S(2)}, u32[]{:S(2)}) collective-permute-start(bf16[2896,128]{1,0:T(8,128)(2,1)S(1)} %collective-permute-done.1.refs_0_), channel_id=1, source_target_pairs={{1,0},{2,3},{5,4},{6,7},{9,8},{10,11},{13,12},{14,15},{17,16},{18,... | collective-permute-start | bytes 2224136 | tf_op jit(solution)/shard_map/ppermute | solution.py:284
  31.3 21.4 %all-to-all-start.1 = ((bf16[8,24,2976]{2,1,0:T(8,128)(2,1)}), bf16[8,24,2976]{2,1,0:T(8,128)(2,1)}, u32[]{:S(2)}, u32[]{:S(2)}) async-start(bf16[8,24,2976]{2,1,0:T(8,128)(2,1)} %get-tuple-element.135), calls=%async_computation.1 | async-start | bytes 2359296 | tf_op jit(solution)/shard_map/all_to_all | solution.py:287
  48.4 21.6 %collective-permute-start.4 = (bf16[2896,128]{1,0:T(8,128)(2,1)}, bf16[2896,128]{1,0:T(8,128)(2,1)S(1)}, u32[]{:S(2)}, u32[]{:S(2)}) collective-permute-start(bf16[2896,128]{1,0:T(8,128)(2,1)} %collective-permute-done.2.refs_0_), channel_id=1, source_target_pairs={{1,0},{2,3},{5,4},{6,7},{9,8},{10,11},{13,12},{14,15},{17,16},{18,... | collective-permute-start | bytes 2224136 | tf_op jit(solution)/shard_map/ppermute | solution.py:284
  52.7 21.2 %all-to-all-start.2 = ((bf16[8,24,2976]{2,1,0:T(8,128)(2,1)}), bf16[8,24,2976]{2,1,0:T(8,128)(2,1)}, u32[]{:S(2)}, u32[]{:S(2)}) async-start(bf16[8,24,2976]{2,1,0:T(8,128)(2,1)} %get-tuple-element.141), calls=%async_computation.2 | async-start | bytes 2359296 | tf_op jit(solution)/shard_map/all_to_all | solution.py:287
  70.1 0.9 copy-start.16
  73.9 27.0 %all-to-all-start.3 = ((bf16[8,24,2976]{2,1,0:T(8,128)(2,1)}), bf16[8,24,2976]{2,1,0:T(8,128)(2,1)}, u32[]{:S(2)}, u32[]{:S(2)}) async-start(bf16[8,24,2976]{2,1,0:T(8,128)(2,1)} %get-tuple-element.150), calls=%async_computation.3 | async-start | bytes 2359296 | tf_op jit(solution)/shard_map/all_to_all | solution.py:287
  91.3 3.9 %collective-permute-start.5 = (bf16[2,24,1444]{2,1,0:T(8,128)(2,1)}, bf16[2,24,1444]{2,1,0:T(8,128)(2,1)S(1)}, u32[]{:S(2)}, u32[]{:S(2)}) collective-permute-start(bf16[2,24,1444]{2,1,0:T(8,128)(2,1)} %get-tuple-element.171), channel_id=1, source_target_pairs={{0,4},{4,0},{8,12},{12,8},{16,20},{20,16},{24,28},{28,24},{1,5},{5... | collective-permute-start | bytes 415880 | tf_op jit(solution)/shard_map/ppermute | solution.py:299
  91.7 5.8 %collective-permute-start.6 = (bf16[2,24,1444]{2,1,0:T(8,128)(2,1)}, bf16[2,24,1444]{2,1,0:T(8,128)(2,1)S(1)}, u32[]{:S(2)}, u32[]{:S(2)}) collective-permute-start(bf16[2,24,1444]{2,1,0:T(8,128)(2,1)} %get-tuple-element.172), channel_id=1, source_target_pairs={{0,8},{4,12},{8,0},{12,4},{16,24},{20,28},{24,16},{28,20},{1,9},{5... | collective-permute-start | bytes 415880 | tf_op jit(solution)/shard_map/ppermute | solution.py:299
  93.1 19.4 %collective-permute-start.7 = (bf16[2,24,1444]{2,1,0:T(8,128)(2,1)}, bf16[2,24,1444]{2,1,0:T(8,128)(2,1)S(1)}, u32[]{:S(2)}, u32[]{:S(2)}) collective-permute-start(bf16[2,24,1444]{2,1,0:T(8,128)(2,1)} %get-tuple-element.173), channel_id=1, source_target_pairs={{0,12},{4,8},{8,4},{12,0},{16,28},{20,24},{24,20},{28,16},{1,13},{... | collective-permute-start | bytes 415880 | tf_op jit(solution)/shard_map/ppermute | solution.py:299
  93.5 19.1 %collective-permute-start.8 = (bf16[2,24,1444]{2,1,0:T(8,128)(2,1)}, bf16[2,24,1444]{2,1,0:T(8,128)(2,1)S(1)}, u32[]{:S(2)}, u32[]{:S(2)}) collective-permute-start(bf16[2,24,1444]{2,1,0:T(8,128)(2,1)} %get-tuple-element.174), channel_id=1, source_target_pairs={{0,16},{4,20},{8,24},{12,28},{16,0},{20,4},{24,8},{28,12},{1,17},{... | collective-permute-start | bytes 415880 | tf_op jit(solution)/shard_map/ppermute | solution.py:299
  94.9 17.7 %collective-permute-start.9 = (bf16[2,24,1444]{2,1,0:T(8,128)(2,1)}, bf16[2,24,1444]{2,1,0:T(8,128)(2,1)S(1)}, u32[]{:S(2)}, u32[]{:S(2)}) collective-permute-start(bf16[2,24,1444]{2,1,0:T(8,128)(2,1)} %get-tuple-element.175), channel_id=1, source_target_pairs={{0,20},{4,16},{8,28},{12,24},{16,4},{20,0},{24,12},{28,8},{1,21},{... | collective-permute-start | bytes 415880 | tf_op jit(solution)/shard_map/ppermute | solution.py:299
  95.2 17.3 %copy-start.1 = (bf16[2,24,1444]{2,1,0:T(8,128)(2,1)}, bf16[2,24,1444]{2,1,0:T(8,128)(2,1)S(1)}, u32[]{:S(2)}) copy-start(bf16[2,24,1444]{2,1,0:T(8,128)(2,1)S(1)} %collective-permute-done.5.refs_1_) | copy-start | bytes 415876
  95.2 17.4 %collective-permute-start.10 = (bf16[2,24,1444]{2,1,0:T(8,128)(2,1)}, bf16[2,24,1444]{2,1,0:T(8,128)(2,1)S(1)}, u32[]{:S(2)}, u32[]{:S(2)}) collective-permute-start(bf16[2,24,1444]{2,1,0:T(8,128)(2,1)} %get-tuple-element.176), channel_id=1, source_target_pairs={{0,24},{4,28},{8,16},{12,20},{16,8},{20,12},{24,0},{28,4},{1,25},{... | collective-permute-start | bytes 415880 | tf_op jit(solution)/shard_map/ppermute | solution.py:299
  97.5 15.0 %copy-start.2 = (bf16[2,24,1444]{2,1,0:T(8,128)(2,1)}, bf16[2,24,1444]{2,1,0:T(8,128)(2,1)S(1)}, u32[]{:S(2)}) copy-start(bf16[2,24,1444]{2,1,0:T(8,128)(2,1)S(1)} %collective-permute-done.6.refs_2_) | copy-start | bytes 415876
  97.5 15.1 %collective-permute-start.11 = (bf16[2,24,1444]{2,1,0:T(8,128)(2,1)}, bf16[2,24,1444]{2,1,0:T(8,128)(2,1)}, u32[]{:S(2)}, u32[]{:S(2)}) collective-permute-start(bf16[2,24,1444]{2,1,0:T(8,128)(2,1)} %get-tuple-element.177), channel_id=1, source_target_pairs={{0,28},{4,24},{8,20},{12,16},{16,12},{20,8},{24,4},{28,0},{1,29},{... | collective-permute-start | bytes 415880 | tf_op jit(solution)/shard_map/ppermute | solution.py:299
  112.5 0.7 copy-start.3
  112.5 0.7 copy-start.4
  112.6 0.7 copy-start.5
  112.6 0.8 copy-start.6
  115.8 21.8 %collective-permute-start.12 = (bf16[128,1444]{1,0:T(8,128)(2,1)}, bf16[128,1444]{1,0:T(8,128)(2,1)S(1)}, u32[]{:S(2)}, u32[]{:S(2)}) collective-permute-start(bf16[128,1444]{1,0:T(8,128)(2,1)} %gather.3), channel_id=1, source_target_pairs={{0,2},{1,3},{2,0},{3,1},{4,6},{5,7},{6,4},{7,5},{8,10},{9,11},{10,... | collective-permute-start | bytes 1109000 | tf_op jit(solution)/shard_map/ppermute | solution.py:284
  120.0 2.4 %collective-permute-start.13 = (bf16[1,24,1444]{2,1,0:T(8,128)(2,1)}, bf16[1,24,1444]{2,1,0:T(8,128)(2,1)S(1)}, u32[]{:S(2)}, u32[]{:S(2)}) collective-permute-start(bf16[1,24,1444]{2,1,0:T(8,128)(2,1)} %get-tuple-element.197), channel_id=1, source_target_pairs={{0,4},{4,0},{8,12},{12,8},{16,20},{20,16},{24,28},{28,24},{1,5},{5... | collective-permute-start | bytes 207944 | tf_op jit(solution)/shard_map/ppermute | solution.py:299
  120.0 3.7 %collective-permute-start.14 = (bf16[1,24,1444]{2,1,0:T(8,128)(2,1)}, bf16[1,24,1444]{2,1,0:T(8,128)(2,1)S(1)}, u32[]{:S(2)}, u32[]{:S(2)}) collective-permute-start(bf16[1,24,1444]{2,1,0:T(8,128)(2,1)} %get-tuple-element.198), channel_id=1, source_target_pairs={{0,8},{4,12},{8,0},{12,4},{16,24},{20,28},{24,16},{28,20},{1,9},{5... | collective-permute-start | bytes 207944 | tf_op jit(solution)/shard_map/ppermute | solution.py:299
  120.3 6.0 %collective-permute-start.15 = (bf16[1,24,1444]{2,1,0:T(8,128)(2,1)}, bf16[1,24,1444]{2,1,0:T(8,128)(2,1)S(1)}, u32[]{:S(2)}, u32[]{:S(2)}) collective-permute-start(bf16[1,24,1444]{2,1,0:T(8,128)(2,1)} %get-tuple-element.199), channel_id=1, source_target_pairs={{0,12},{4,8},{8,4},{12,0},{16,28},{20,24},{24,20},{28,16},{1,13},{... | collective-permute-start | bytes 207944 | tf_op jit(solution)/shard_map/ppermute | solution.py:299
  122.1 8.7 %collective-permute-start.16 = (bf16[1,24,1444]{2,1,0:T(8,128)(2,1)}, bf16[1,24,1444]{2,1,0:T(8,128)(2,1)S(1)}, u32[]{:S(2)}, u32[]{:S(2)}) collective-permute-start(bf16[1,24,1444]{2,1,0:T(8,128)(2,1)} %get-tuple-element.200), channel_id=1, source_target_pairs={{0,16},{4,20},{8,24},{12,28},{16,0},{20,4},{24,8},{28,12},{1,17},{... | collective-permute-start | bytes 207944 | tf_op jit(solution)/shard_map/ppermute | solution.py:299
  122.4 9.6 %copy-start.8 = (bf16[1,24,1444]{2,1,0:T(8,128)(2,1)}, bf16[1,24,1444]{2,1,0:T(8,128)(2,1)S(1)}, u32[]{:S(2)}) copy-start(bf16[1,24,1444]{2,1,0:T(8,128)(2,1)S(1)} %collective-permute-done.13.refs_1_) | copy-start | bytes 207940
  122.4 8.5 %collective-permute-start.17 = (bf16[1,24,1444]{2,1,0:T(8,128)(2,1)}, bf16[1,24,1444]{2,1,0:T(8,128)(2,1)S(1)}, u32[]{:S(2)}, u32[]{:S(2)}) collective-permute-start(bf16[1,24,1444]{2,1,0:T(8,128)(2,1)} %get-tuple-element.201), channel_id=1, source_target_pairs={{0,20},{4,16},{8,28},{12,24},{16,4},{20,0},{24,12},{28,8},{1,21},{... | collective-permute-start | bytes 207944 | tf_op jit(solution)/shard_map/ppermute | solution.py:299
  123.7 8.3 %copy-start.9 = (bf16[1,24,1444]{2,1,0:T(8,128)(2,1)}, bf16[1,24,1444]{2,1,0:T(8,128)(2,1)S(1)}, u32[]{:S(2)}) copy-start(bf16[1,24,1444]{2,1,0:T(8,128)(2,1)S(1)} %collective-permute-done.14.refs_2_) | copy-start | bytes 207940
  123.7 7.2 %collective-permute-start.18 = (bf16[1,24,1444]{2,1,0:T(8,128)(2,1)}, bf16[1,24,1444]{2,1,0:T(8,128)(2,1)S(1)}, u32[]{:S(2)}, u32[]{:S(2)}) collective-permute-start(bf16[1,24,1444]{2,1,0:T(8,128)(2,1)} %get-tuple-element.202), channel_id=1, source_target_pairs={{0,24},{4,28},{8,16},{12,20},{16,8},{20,12},{24,0},{28,4},{1,25},{... | collective-permute-start | bytes 207944 | tf_op jit(solution)/shard_map/ppermute | solution.py:299
  126.2 5.8 %copy-start.10 = (bf16[1,24,1444]{2,1,0:T(8,128)(2,1)}, bf16[1,24,1444]{2,1,0:T(8,128)(2,1)S(1)}, u32[]{:S(2)}) copy-start(bf16[1,24,1444]{2,1,0:T(8,128)(2,1)S(1)} %collective-permute-done.15.refs_3_) | copy-start | bytes 207940
  126.2 5.8 %collective-permute-start.19 = (bf16[1,24,1444]{2,1,0:T(8,128)(2,1)}, bf16[1,24,1444]{2,1,0:T(8,128)(2,1)S(1)}, u32[]{:S(2)}, u32[]{:S(2)}) collective-permute-start(bf16[1,24,1444]{2,1,0:T(8,128)(2,1)} %get-tuple-element.203), channel_id=1, source_target_pairs={{0,28},{4,24},{8,20},{12,16},{16,12},{20,8},{24,4},{28,0},{1,29},{... | collective-permute-start | bytes 207944 | tf_op jit(solution)/shard_map/ppermute | solution.py:299
  130.8 1.2 copy-start.11
  130.8 27.5 %collective-permute-start.20 = (bf16[128,1444]{1,0:T(8,128)(2,1)}, bf16[128,1444]{1,0:T(8,128)(2,1)}, u32[]{:S(2)}, u32[]{:S(2)}) collective-permute-start(bf16[128,1444]{1,0:T(8,128)(2,1)} %gather.4), channel_id=1, source_target_pairs={{0,1},{1,0},{2,3},{3,2},{4,5},{5,4},{6,7},{7,6},{8,9},{9,8},{10,11... | collective-permute-start | bytes 1109000 | tf_op jit(solution)/shard_map/ppermute | solution.py:284
  130.9 1.1 copy-start.12
  130.9 1.1 copy-start.13
  132.0 0.6 copy-start.14
  134.9 23.5 %collective-permute-start.21 = (bf16[128,1444]{1,0:T(8,128)(2,1)}, bf16[128,1444]{1,0:T(8,128)(2,1)}, u32[]{:S(2)}, u32[]{:S(2)}) collective-permute-start(bf16[128,1444]{1,0:T(8,128)(2,1)} %gather.5), channel_id=1, source_target_pairs={{0,3},{1,2},{2,1},{3,0},{4,7},{5,6},{6,5},{7,4},{8,11},{9,10},{10,... | collective-permute-start | bytes 1109000 | tf_op jit(solution)/shard_map/ppermute | solution.py:284
  137.6 20.8 %copy-start.7 = (bf16[128,1444]{1,0:T(8,128)(2,1)}, bf16[128,1444]{1,0:T(8,128)(2,1)S(1)}, u32[]{:S(2)}) copy-start(bf16[128,1444]{1,0:T(8,128)(2,1)S(1)} %collective-permute-done.12.refs_1_) | copy-start | bytes 1108996
  137.6 20.8 %all-to-all-start.4 = ((bf16[8,1,24,1444]{3,2,1,0:T(8,128)(2,1)}), bf16[8,1,24,1444]{3,2,1,0:T(8,128)(2,1)S(1)}, u32[]{:S(2)}, u32[]{:S(2)}) async-start(bf16[8,1,24,1444]{3,2,1,0:T(8,128)(2,1)} %get-tuple-element.217), calls=%async_computation.4 | async-start | bytes 1179648 | tf_op jit(solution)/shard_map/all_to_all | solution.py:287
  158.4 0.8 copy-start

commit v3 on v2

--- a/solution.py
+++ b/solution.py
@@ -249,7 +249,7 @@
     gd_ref[0] = dot(a, ys, 0, 0).astype(BF)
 
 
-def weight_grads(x, dh, du, a, ys, step=256):
+def weight_grads(x, dh, du, a, ys, step=384):
     width, hidden = ys[0].shape[1], a[0].shape[1]
     rows = sum(v.shape[0] for v in x)
     cols = lambda vs: [pl.BlockSpec((v.shape[0], step), lambda i: (0, i)) for v in vs]
@@ -296,8 +296,9 @@
         return expert(place, got, wg, wu, wd, width, lane, topk, n, islands, prev, fan)
 
     def give(rets):
-        return [rets[0]] + [lax.ppermute(rets[j], "island", [(i, i ^ j) for i in range(islands)])
-                            for j in range(1, islands)]
+        sent = {j: lax.ppermute(rets[j], "island", [(i, i ^ j) for i in range(islands)])
+                for j in reversed(range(1, islands))}
+        return [rets[0]] + [sent[j] for j in range(1, islands)]
 
     def part(total, s):
         return send(total, [(i, i ^ s) for i in range(n)])

time: 163 us -> 162 us (level)
  no operation moved by 1% of the time
where the time goes in v3:
time: 162 us
  Pallas kernels  85.1 us (53%)
  starting transfers between devices  56.1 us (35%)
  waiting for transfers between devices  15.7 us (10%)
  local copies, waits for them, and re-layouts  3.06 us (2%)
    pallas_call x4, Pallas kernels, expert(): pl.pallas_call(functools.partial(expert_kernel, width, hidden, lane, topk...  46.4 us
    all_to_all x5, starting transfers between devices, a2a(): return lax.all_to_all(v, 'island', 0, 0, tiled=True)  25.3 us
    pallas_call x1, Pallas kernels, weight_grads(): pl.pallas_call(functools.partial(weights_kernel, [len(v) for v in (x, dh,...  17.2 us
    ppermute x14, starting transfers between devices, give(): lax.ppermute(rets[j], 'island', [(i, i ^ j) for i in range(islands)])  15.9 us
    ppermute x8, starting transfers between devices, send(): return lax.ppermute(v, 'local', pairs)  14.9 us
    ppermute x8, waiting for transfers between devices, send(): return lax.ppermute(v, 'local', pairs)  12.5 us
    pallas_call x3, Pallas kernels, pick(): pl.pallas_call(functools.partial(pick_kernel, width, meta, lane, islands,...  8.71 us
    pallas_call x3, Pallas kernels, gather(): pl.pallas_call(functools.partial(gather_kernel, at), out_shape=jax.ShapeD...  7.4 us
  transfers between devices with their start and end apart: 27, of which 6 were waited for; matrix products, arithmetic and copies ran while one was open for 0% of the time, Pallas kernels for 48%

profile of v3, /device:TPU:1, one launch (start us, length us, event | category | flops | bytes accessed | tf_op | source)
XLA Modules:
  0.0 161.5 jit_solution(11861859908974954033)
XLA Ops:
  0.6 0.7 pad_add_fusion.place_ref
  1.3 2.8 %pack.1 = (bf16[2896,128]{1,0:T(8,128)(2,1)}, bf16[8,24,2976]{2,1,0:T(8,128)(2,1)}, bf16[192,128]{1,0:T(8,128)(2,1)}) custom-call(s32[3]{0:T(128)} %pad_add_fusion.place_ref, bf16[1440,128]{1,0:T(8,128)(2,1)} %bitcast.28, bf16[4,128]{1,0:T(4,128)(2,1)} %bitcast.31, s32[4,128]{1,0:T(4,128)} %bitcast.30, bf16[1440,128]{1,0:T(8,128)(2,1)} %bitcast.29), custom_call_target="tpu_custom_call" | custom-call | flops 1048576 | bytes 65536 | tf_op jit(solution)/shard_map/pack/pallas_call | solution.py:231
  4.1 0.7 collective-permute-start.1
  4.8 4.7 %collective-permute-start = (bf16[2896,128]{1,0:T(8,128)(2,1)}, bf16[2896,128]{1,0:T(8,128)(2,1)}, u32[]{:S(2)}, u32[]{:S(2)}) collective-permute-start(bf16[2896,128]{1,0:T(8,128)(2,1)} %get-tuple-element.125), channel_id=1, source_target_pairs={{0,1},{1,0},{2,3},{3,2},{4,5},{5,4},{6,7},{7,6},{8,9},{9,8},{10,11... | collective-permute-start | bytes 2224136 | tf_op jit(solution)/shard_map/ppermute | solution.py:284
  9.5 5.4 %all-to-all-start = ((bf16[8,24,2976]{2,1,0:T(8,128)(2,1)}), bf16[8,24,2976]{2,1,0:T(8,128)(2,1)}, u32[]{:S(2)}, u32[]{:S(2)}) async-start(bf16[8,24,2976]{2,1,0:T(8,128)(2,1)} %get-tuple-element.128), calls=%async_computation | async-start | bytes 2359296 | tf_op jit(solution)/shard_map/all_to_all | solution.py:287
  14.8 10.9 %collective-permute-done.refs_0_ = bf16[2896,128]{1,0:T(8,128)(2,1)} collective-permute-done((bf16[2896,128]{1,0:T(8,128)(2,1)}, bf16[2896,128]{1,0:T(8,128)(2,1)}, u32[]{:S(2)}, u32[]{:S(2)}) %collective-permute-start) | collective-permute-done | bytes 741408 | tf_op jit(solution)/shard_map/ppermute | solution.py:284
  25.8 1.5 collective-permute-start.2
  27.3 1.3 collective-permute-start.3
  28.6 2.8 %pick.3 = (bf16[8,24,2976]{2,1,0:T(8,128)(2,1)}, bf16[192,128]{1,0:T(8,128)(2,1)}) custom-call(s32[3]{0:T(128)} %pad_add_fusion.place_ref, bf16[2896,128]{1,0:T(8,128)(2,1)} %collective-permute-done.refs_0_), custom_call_target="tpu_custom_call" | custom-call | flops 12000000000 | bytes 1048576 | tf_op jit(solution)/shard_map/pick/pallas_call | solution.py:88
  31.3 5.7 %all-to-all-start.1 = ((bf16[8,24,2976]{2,1,0:T(8,128)(2,1)}), bf16[8,24,2976]{2,1,0:T(8,128)(2,1)}, u32[]{:S(2)}, u32[]{:S(2)}) async-start(bf16[8,24,2976]{2,1,0:T(8,128)(2,1)} %get-tuple-element.135), calls=%async_computation.1 | async-start | bytes 2359296 | tf_op jit(solution)/shard_map/all_to_all | solution.py:287
  37.0 11.4 %expert.4 = (bf16[8,1,24,1444]{3,2,1,0:T(8,128)(2,1)}, bf16[192,1440]{1,0:T(8,128)(2,1)}, bf16[192,1440]{1,0:T(8,128)(2,1)}, bf16[192,1440]{1,0:T(8,128)(2,1)}, bf16[192,1440]{1,0:T(8,128)(2,1)}) custom-call(s32[3]{0:T(128)} %pad_add_fusion.place_ref, bf16[192,2976]{1,0:T(8,128)(2,1)} %bitcast.7.got_ref.refs_0_, bf16[1440,1440]{1,0:T(8,128)(2,1)} %bitcast.16, ...), custom_call_target="tpu_custom_call" | custom-call | flops 1048576 | bytes 65536 | tf_op jit(solution)/shard_map/expert/pallas_call | solution.py:161
  48.4 1.3 collective-permute-start.4
  49.7 3.0 %pick.4 = (bf16[8,24,2976]{2,1,0:T(8,128)(2,1)}, bf16[192,128]{1,0:T(8,128)(2,1)}) custom-call(s32[3]{0:T(128)} %pad_add_fusion.place_ref, bf16[2896,128]{1,0:T(8,128)(2,1)} %collective-permute-done.2.refs_0_, bf16[2896,128]{1,0:T(8,128)(2,1)} %collective-permute-done.3.refs_1_), custom_call_target="tpu_custom_call" | custom-call | flops 12000000000 | bytes 1048576 | tf_op jit(solution)/shard_map/pick/pallas_call | solution.py:88
  52.7 5.4 %all-to-all-start.2 = ((bf16[8,24,2976]{2,1,0:T(8,128)(2,1)}), bf16[8,24,2976]{2,1,0:T(8,128)(2,1)}, u32[]{:S(2)}, u32[]{:S(2)}) async-start(bf16[8,24,2976]{2,1,0:T(8,128)(2,1)} %get-tuple-element.141), calls=%async_computation.2 | async-start | bytes 2359296 | tf_op jit(solution)/shard_map/all_to_all | solution.py:287
  58.1 11.4 %expert.5 = (bf16[8,1,24,1444]{3,2,1,0:T(8,128)(2,1)}, bf16[192,1440]{1,0:T(8,128)(2,1)}, bf16[192,1440]{1,0:T(8,128)(2,1)}, bf16[192,1440]{1,0:T(8,128)(2,1)}, bf16[192,1440]{1,0:T(8,128)(2,1)}) custom-call(s32[3]{0:T(128)} %pad_add_fusion.place_ref, bf16[192,2976]{1,0:T(8,128)(2,1)} %bitcast.11.got_ref.refs_1_, bf16[1440,1440]{1,0:T(8,128)(2,1)} %bitcast.17, ...), custom_call_target="tpu_custom_call" | custom-call | flops 1048576 | bytes 65536 | tf_op jit(solution)/shard_map/expert/pallas_call | solution.py:161
  69.5 0.6 collective-permute-done.4.refs_1_
  70.1 0.9 copy-done.16
  70.9 3.0 %pick.5 = (bf16[8,24,2976]{2,1,0:T(8,128)(2,1)}, bf16[192,128]{1,0:T(8,128)(2,1)}) custom-call(s32[3]{0:T(128)} %pad_add_fusion.place_ref, bf16[2896,128]{1,0:T(8,128)(2,1)} %copy-done.15, bf16[2896,128]{1,0:T(8,128)(2,1)} %copy-done.16), custom_call_target="tpu_custom_call" | custom-call | flops 12000000000 | bytes 1048576 | tf_op jit(solution)/shard_map/pick/pallas_call | solution.py:88
  73.9 5.3 %all-to-all-start.3 = ((bf16[8,24,2976]{2,1,0:T(8,128)(2,1)}), bf16[8,24,2976]{2,1,0:T(8,128)(2,1)}, u32[]{:S(2)}, u32[]{:S(2)}) async-start(bf16[8,24,2976]{2,1,0:T(8,128)(2,1)} %get-tuple-element.150), calls=%async_computation.3 | async-start | bytes 2359296 | tf_op jit(solution)/shard_map/all_to_all | solution.py:287
  79.2 12.1 %expert.6 = (bf16[2,24,1444]{2,1,0:T(8,128)(2,1)}, bf16[2,24,1444]{2,1,0:T(8,128)(2,1)}, bf16[2,24,1444]{2,1,0:T(8,128)(2,1)}, bf16[2,24,1444]{2,1,0:T(8,128)(2,...) custom-call(s32[3]{0:T(128)} %pad_add_fusion.place_ref, ...), custom_call_target="tpu_custom_call" | custom-call | flops 1048576 | bytes 65536 | tf_op jit(solution)/shard_map/expert/pallas_call | solution.py:161
  91.3 0.4 collective-permute-start.5
  91.7 1.4 collective-permute-start.6
  93.1 0.4 collective-permute-start.7
  93.5 1.4 collective-permute-start.8
  94.9 0.3 collective-permute-start.9
  95.2 2.3 %collective-permute-start.10 = (bf16[2,24,1444]{2,1,0:T(8,128)(2,1)}, bf16[2,24,1444]{2,1,0:T(8,128)(2,1)S(1)}, u32[]{:S(2)}, u32[]{:S(2)}) collective-permute-start(bf16[2,24,1444]{2,1,0:T(8,128)(2,1)} %get-tuple-element.176), channel_id=1, source_target_pairs={{0,24},{4,28},{8,16},{12,20},{16,8},{20,12},{24,0},{28,4},{1,25},{... | collective-permute-start | bytes 415880 | tf_op jit(solution)/shard_map/ppermute | solution.py:299
  97.5 3.4 %collective-permute-start.11 = (bf16[2,24,1444]{2,1,0:T(8,128)(2,1)}, bf16[2,24,1444]{2,1,0:T(8,128)(2,1)}, u32[]{:S(2)}, u32[]{:S(2)}) collective-permute-start(bf16[2,24,1444]{2,1,0:T(8,128)(2,1)} %get-tuple-element.177), channel_id=1, source_target_pairs={{0,28},{4,24},{8,20},{12,16},{16,12},{20,8},{24,4},{28,0},{1,29},{... | collective-permute-start | bytes 415880 | tf_op jit(solution)/shard_map/ppermute | solution.py:299
  100.9 11.6 %expert.7 = (bf16[1,24,1444]{2,1,0:T(8,128)(2,1)}, bf16[1,24,1444]{2,1,0:T(8,128)(2,1)}, bf16[1,24,1444]{2,1,0:T(8,128)(2,1)}, bf16[1,24,1444]{2,1,0:T(8,128)(2,...) custom-call(s32[3]{0:T(128)} %pad_add_fusion.place_ref, ...), custom_call_target="tpu_custom_call" | custom-call | flops 1048576 | bytes 65536 | tf_op jit(solution)/shard_map/expert/pallas_call | solution.py:161
  112.6 0.6 copy-done.3
  113.3 2.4 %gather.3 = bf16[128,1444]{1,0:T(8,128)(2,1)} custom-call(s32[3]{0:T(128)} %pad_add_fusion.place_ref, bf16[192,128]{1,0:T(8,128)(2,1)} %get-tuple-element.134.hot_ref, bf16[2,24,1444]{2,1,0:T(8,128)(2,1)} %get-tuple-element.178.refs_0_, bf16[2,24,1444]{2,1,0:T(8,128)(2,1)} %copy-done.1, bf16[2,24,1444]{2,1,0:T(8,128)(2,1)} %copy-done.2, ...), custom_call_target="tpu_custom_call" | custom-call | flops 1048576 | bytes 65536 | tf_op jit(solution)/shard_map/gather/pallas_call | solution.py:198
  115.8 4.2 %collective-permute-start.12 = (bf16[128,1444]{1,0:T(8,128)(2,1)}, bf16[128,1444]{1,0:T(8,128)(2,1)S(1)}, u32[]{:S(2)}, u32[]{:S(2)}) collective-permute-start(bf16[128,1444]{1,0:T(8,128)(2,1)} %gather.3), channel_id=1, source_target_pairs={{0,2},{1,3},{2,0},{3,1},{4,6},{5,7},{6,4},{7,5},{8,10},{9,11},{10,... | collective-permute-start | bytes 1109000 | tf_op jit(solution)/shard_map/ppermute | solution.py:284
  120.0 0.3 collective-permute-start.14
  120.3 1.8 %collective-permute-start.15 = (bf16[1,24,1444]{2,1,0:T(8,128)(2,1)}, bf16[1,24,1444]{2,1,0:T(8,128)(2,1)S(1)}, u32[]{:S(2)}, u32[]{:S(2)}) collective-permute-start(bf16[1,24,1444]{2,1,0:T(8,128)(2,1)} %get-tuple-element.199), channel_id=1, source_target_pairs={{0,12},{4,8},{8,4},{12,0},{16,28},{20,24},{24,20},{28,16},{1,13},{... | collective-permute-start | bytes 207944 | tf_op jit(solution)/shard_map/ppermute | solution.py:299
  122.1 0.3 collective-permute-start.16
  122.4 1.1 collective-permute-start.17
  123.7 0.7 collective-permute-start.18
  124.4 1.9 %collective-permute-done.15.refs_3_ = bf16[1,24,1444]{2,1,0:T(8,128)(2,1)S(1)} collective-permute-done((bf16[1,24,1444]{2,1,0:T(8,128)(2,1)}, bf16[1,24,1444]{2,1,0:T(8,128)(2,1)S(1)}, u32[]{:S(2)}, u32[]{:S(2)}) %collective-permute-start.15) | collective-permute-done | bytes 69344 | tf_op jit(solution)/shard_map/ppermute | solution.py:299
  126.2 2.1 %collective-permute-start.19 = (bf16[1,24,1444]{2,1,0:T(8,128)(2,1)}, bf16[1,24,1444]{2,1,0:T(8,128)(2,1)S(1)}, u32[]{:S(2)}, u32[]{:S(2)}) collective-permute-start(bf16[1,24,1444]{2,1,0:T(8,128)(2,1)} %get-tuple-element.203), channel_id=1, source_target_pairs={{0,28},{4,24},{8,20},{12,16},{16,12},{20,8},{24,4},{28,0},{1,29},{... | collective-permute-start | bytes 207944 | tf_op jit(solution)/shard_map/ppermute | solution.py:299
  128.4 2.4 %gather.4 = bf16[128,1444]{1,0:T(8,128)(2,1)} custom-call(s32[3]{0:T(128)} %pad_add_fusion.place_ref, bf16[192,128]{1,0:T(8,128)(2,1)} %get-tuple-element.187.hot_ref, bf16[2,24,1444]{2,1,0:T(8,128)(2,1)} %get-tuple-element.178.refs_0_, bf16[2,24,1444]{2,1,0:T(8,128)(2,1)} %copy-done.1, bf16[2,24,1444]{2,1,0:T(8,128)(2,1)} %copy-done.2, ...), custom_call_target="tpu_custom_call" | custom-call | flops 1048576 | bytes 65536 | tf_op jit(solution)/shard_map/gather/pallas_call | solution.py:198
  131.0 1.0 collective-permute-done.19.refs_7_
  132.0 0.6 copy-done.14
  132.6 2.5 %gather.5 = bf16[128,1444]{1,0:T(8,128)(2,1)} custom-call(s32[3]{0:T(128)} %pad_add_fusion.place_ref, bf16[192,128]{1,0:T(8,128)(2,1)} %get-tuple-element.186.hot_ref, bf16[1,24,1444]{2,1,0:T(8,128)(2,1)} %get-tuple-element.204.refs_0_, bf16[1,24,1444]{2,1,0:T(8,128)(2,1)} %copy-done.8, bf16[1,24,1444]{2,1,0:T(8,128)(2,1)} %copy-done.9, ...), custom_call_target="tpu_custom_call" | custom-call | flops 1048576 | bytes 65536 | tf_op jit(solution)/shard_map/gather/pallas_call | solution.py:198
  135.1 1.1 collective-permute-start.21
  136.3 1.0 collective-permute-done.12.refs_1_
  137.3 3.5 %all-to-all-start.4 = ((bf16[8,1,24,1444]{3,2,1,0:T(8,128)(2,1)}), bf16[8,1,24,1444]{3,2,1,0:T(8,128)(2,1)S(1)}, u32[]{:S(2)}, u32[]{:S(2)}) async-start(bf16[8,1,24,1444]{3,2,1,0:T(8,128)(2,1)} %get-tuple-element.217), calls=%async_computation.4 | async-start | bytes 1179648 | tf_op jit(solution)/shard_map/all_to_all | solution.py:287
  140.8 17.2 %weight_grads.1 = (bf16[1,1440,1440]{2,1,0:T(8,128)(2,1)}, bf16[1,1440,1440]{2,1,0:T(8,128)(2,1)}, bf16[1,1440,1440]{2,1,0:T(8,128)(2,1)}) custom-call(bf16[192,2976]{1,0:T(8,128)(2,1)} %bitcast.7.got_ref.refs_0_, bf16[192,2976]{1,0:T(8,128)(2,1)} %bitcast.11.got_ref.refs_1_, bf16[192,2976]{1,0:T(8,128)(2,1)} %bitcast.12.got_ref.refs_2_, ...), custom_call_target="tpu_custom_call" | custom-call | flops 12000000000 | bytes 1048576 | tf_op jit(solution)/shard_map/weight_grads/pallas_call | solution.py:258
  158.1 0.8 copy-done
  158.9 2.6 %merge.1 = (bf16[1440,128]{1,0:T(8,128)(2,1)}, bf16[4,128]{1,0:T(4,128)(2,1)}) custom-call(bf16[192,128]{1,0:T(8,128)(2,1)} %get-tuple-element.124.hot_ref, bf16[8,1,24,1444]{3,2,1,0:T(8,128)(2,1)} %copy-done, bf16[128,1444]{1,0:T(8,128)(2,1)} %collective-permute-done.20.refs_0_, bf16[128,1444]{1,0:T(8,128)(2,1)} %copy-done.7, ...), custom_call_target="tpu_custom_call" | custom-call | flops 1048576 | bytes 65536 | tf_op jit(solution)/shard_map/merge/pallas_call | solution.py:209
  (54 shorter events, 0.5 us)
Async XLA Ops:
  4.1 10.8 %collective-permute-start.1 = (bf16[2896,128]{1,0:T(8,128)(2,1)}, bf16[2896,128]{1,0:T(8,128)(2,1)S(1)}, u32[]{:S(2)}, u32[]{:S(2)}) collective-permute-start(bf16[2896,128]{1,0:T(8,128)(2,1)} %get-tuple-element.125), channel_id=1, source_target_pairs={{1,2},{2,1},{5,6},{6,5},{9,10},{10,9},{13,14},{14,13},{17,18},{18,... | collective-permute-start | bytes 2224136 | tf_op jit(solution)/shard_map/ppermute | solution.py:284
  4.8 21.0 %collective-permute-start = (bf16[2896,128]{1,0:T(8,128)(2,1)}, bf16[2896,128]{1,0:T(8,128)(2,1)}, u32[]{:S(2)}, u32[]{:S(2)}) collective-permute-start(bf16[2896,128]{1,0:T(8,128)(2,1)} %get-tuple-element.125), channel_id=1, source_target_pairs={{0,1},{1,0},{2,3},{3,2},{4,5},{5,4},{6,7},{7,6},{8,9},{9,8},{10,11... | collective-permute-start | bytes 2224136 | tf_op jit(solution)/shard_map/ppermute | solution.py:284
  9.5 21.9 %all-to-all-start = ((bf16[8,24,2976]{2,1,0:T(8,128)(2,1)}), bf16[8,24,2976]{2,1,0:T(8,128)(2,1)}, u32[]{:S(2)}, u32[]{:S(2)}) async-start(bf16[8,24,2976]{2,1,0:T(8,128)(2,1)} %get-tuple-element.128), calls=%async_computation | async-start | bytes 2359296 | tf_op jit(solution)/shard_map/all_to_all | solution.py:287
  14.8 16.5 %copy-start.15 = (bf16[2896,128]{1,0:T(8,128)(2,1)}, bf16[2896,128]{1,0:T(8,128)(2,1)S(1)}, u32[]{:S(2)}) copy-start(bf16[2896,128]{1,0:T(8,128)(2,1)S(1)} %collective-permute-done.1.refs_0_) | copy-start | bytes 2224132
  25.8 22.6 %collective-permute-start.2 = (bf16[2896,128]{1,0:T(8,128)(2,1)}, bf16[2896,128]{1,0:T(8,128)(2,1)}, u32[]{:S(2)}, u32[]{:S(2)}) collective-permute-start(bf16[2896,128]{1,0:T(8,128)(2,1)} %collective-permute-done.refs_0_), channel_id=1, source_target_pairs={{1,2},{2,1},{5,6},{6,5},{9,10},{10,9},{13,14},{14,13},{17,18},{18,... | collective-permute-start | bytes 2224136 | tf_op jit(solution)/shard_map/ppermute | solution.py:284
  27.3 21.1 %collective-permute-start.3 = (bf16[2896,128]{1,0:T(8,128)(2,1)S(1)}, bf16[2896,128]{1,0:T(8,128)(2,1)}, u32[]{:S(2)}, u32[]{:S(2)}) collective-permute-start(bf16[2896,128]{1,0:T(8,128)(2,1)S(1)} %collective-permute-done.1.refs_0_), channel_id=1, source_target_pairs={{1,0},{2,3},{5,4},{6,7},{9,8},{10,11},{13,12},{14,15},{17,16},{18,... | collective-permute-start | bytes 2224136 | tf_op jit(solution)/shard_map/ppermute | solution.py:284
  31.3 21.4 %all-to-all-start.1 = ((bf16[8,24,2976]{2,1,0:T(8,128)(2,1)}), bf16[8,24,2976]{2,1,0:T(8,128)(2,1)}, u32[]{:S(2)}, u32[]{:S(2)}) async-start(bf16[8,24,2976]{2,1,0:T(8,128)(2,1)} %get-tuple-element.135), calls=%async_computation.1 | async-start | bytes 2359296 | tf_op jit(solution)/shard_map/all_to_all | solution.py:287
  48.4 21.6 %collective-permute-start.4 = (bf16[2896,128]{1,0:T(8,128)(2,1)}, bf16[2896,128]{1,0:T(8,128)(2,1)S(1)}, u32[]{:S(2)}, u32[]{:S(2)}) collective-permute-start(bf16[2896,128]{1,0:T(8,128)(2,1)} %collective-permute-done.2.refs_0_), channel_id=1, source_target_pairs={{1,0},{2,3},{5,4},{6,7},{9,8},{10,11},{13,12},{14,15},{17,16},{18,... | collective-permute-start | bytes 2224136 | tf_op jit(solution)/shard_map/ppermute | solution.py:284
  52.7 21.2 %all-to-all-start.2 = ((bf16[8,24,2976]{2,1,0:T(8,128)(2,1)}), bf16[8,24,2976]{2,1,0:T(8,128)(2,1)}, u32[]{:S(2)}, u32[]{:S(2)}) async-start(bf16[8,24,2976]{2,1,0:T(8,128)(2,1)} %get-tuple-element.141), calls=%async_computation.2 | async-start | bytes 2359296 | tf_op jit(solution)/shard_map/all_to_all | solution.py:287
  70.1 0.9 copy-start.16
  73.9 27.0 %all-to-all-start.3 = ((bf16[8,24,2976]{2,1,0:T(8,128)(2,1)}), bf16[8,24,2976]{2,1,0:T(8,128)(2,1)}, u32[]{:S(2)}, u32[]{:S(2)}) async-start(bf16[8,24,2976]{2,1,0:T(8,128)(2,1)} %get-tuple-element.150), calls=%async_computation.3 | async-start | bytes 2359296 | tf_op jit(solution)/shard_map/all_to_all | solution.py:287
  91.3 3.9 %collective-permute-start.5 = (bf16[2,24,1444]{2,1,0:T(8,128)(2,1)}, bf16[2,24,1444]{2,1,0:T(8,128)(2,1)S(1)}, u32[]{:S(2)}, u32[]{:S(2)}) collective-permute-start(bf16[2,24,1444]{2,1,0:T(8,128)(2,1)} %get-tuple-element.171), channel_id=1, source_target_pairs={{0,4},{4,0},{8,12},{12,8},{16,20},{20,16},{24,28},{28,24},{1,5},{5... | collective-permute-start | bytes 415880 | tf_op jit(solution)/shard_map/ppermute | solution.py:299
  91.7 5.8 %collective-permute-start.6 = (bf16[2,24,1444]{2,1,0:T(8,128)(2,1)}, bf16[2,24,1444]{2,1,0:T(8,128)(2,1)S(1)}, u32[]{:S(2)}, u32[]{:S(2)}) collective-permute-start(bf16[2,24,1444]{2,1,0:T(8,128)(2,1)} %get-tuple-element.172), channel_id=1, source_target_pairs={{0,8},{4,12},{8,0},{12,4},{16,24},{20,28},{24,16},{28,20},{1,9},{5... | collective-permute-start | bytes 415880 | tf_op jit(solution)/shard_map/ppermute | solution.py:299
  93.1 19.4 %collective-permute-start.7 = (bf16[2,24,1444]{2,1,0:T(8,128)(2,1)}, bf16[2,24,1444]{2,1,0:T(8,128)(2,1)S(1)}, u32[]{:S(2)}, u32[]{:S(2)}) collective-permute-start(bf16[2,24,1444]{2,1,0:T(8,128)(2,1)} %get-tuple-element.173), channel_id=1, source_target_pairs={{0,12},{4,8},{8,4},{12,0},{16,28},{20,24},{24,20},{28,16},{1,13},{... | collective-permute-start | bytes 415880 | tf_op jit(solution)/shard_map/ppermute | solution.py:299
  93.5 19.1 %collective-permute-start.8 = (bf16[2,24,1444]{2,1,0:T(8,128)(2,1)}, bf16[2,24,1444]{2,1,0:T(8,128)(2,1)S(1)}, u32[]{:S(2)}, u32[]{:S(2)}) collective-permute-start(bf16[2,24,1444]{2,1,0:T(8,128)(2,1)} %get-tuple-element.174), channel_id=1, source_target_pairs={{0,16},{4,20},{8,24},{12,28},{16,0},{20,4},{24,8},{28,12},{1,17},{... | collective-permute-start | bytes 415880 | tf_op jit(solution)/shard_map/ppermute | solution.py:299
  94.9 17.7 %collective-permute-start.9 = (bf16[2,24,1444]{2,1,0:T(8,128)(2,1)}, bf16[2,24,1444]{2,1,0:T(8,128)(2,1)S(1)}, u32[]{:S(2)}, u32[]{:S(2)}) collective-permute-start(bf16[2,24,1444]{2,1,0:T(8,128)(2,1)} %get-tuple-element.175), channel_id=1, source_target_pairs={{0,20},{4,16},{8,28},{12,24},{16,4},{20,0},{24,12},{28,8},{1,21},{... | collective-permute-start | bytes 415880 | tf_op jit(solution)/shard_map/ppermute | solution.py:299
  95.2 17.3 %copy-start.1 = (bf16[2,24,1444]{2,1,0:T(8,128)(2,1)}, bf16[2,24,1444]{2,1,0:T(8,128)(2,1)S(1)}, u32[]{:S(2)}) copy-start(bf16[2,24,1444]{2,1,0:T(8,128)(2,1)S(1)} %collective-permute-done.5.refs_1_) | copy-start | bytes 415876
  95.2 17.4 %collective-permute-start.10 = (bf16[2,24,1444]{2,1,0:T(8,128)(2,1)}, bf16[2,24,1444]{2,1,0:T(8,128)(2,1)S(1)}, u32[]{:S(2)}, u32[]{:S(2)}) collective-permute-start(bf16[2,24,1444]{2,1,0:T(8,128)(2,1)} %get-tuple-element.176), channel_id=1, source_target_pairs={{0,24},{4,28},{8,16},{12,20},{16,8},{20,12},{24,0},{28,4},{1,25},{... | collective-permute-start | bytes 415880 | tf_op jit(solution)/shard_map/ppermute | solution.py:299
  97.5 15.0 %copy-start.2 = (bf16[2,24,1444]{2,1,0:T(8,128)(2,1)}, bf16[2,24,1444]{2,1,0:T(8,128)(2,1)S(1)}, u32[]{:S(2)}) copy-start(bf16[2,24,1444]{2,1,0:T(8,128)(2,1)S(1)} %collective-permute-done.6.refs_2_) | copy-start | bytes 415876
  97.5 15.1 %collective-permute-start.11 = (bf16[2,24,1444]{2,1,0:T(8,128)(2,1)}, bf16[2,24,1444]{2,1,0:T(8,128)(2,1)}, u32[]{:S(2)}, u32[]{:S(2)}) collective-permute-start(bf16[2,24,1444]{2,1,0:T(8,128)(2,1)} %get-tuple-element.177), channel_id=1, source_target_pairs={{0,28},{4,24},{8,20},{12,16},{16,12},{20,8},{24,4},{28,0},{1,29},{... | collective-permute-start | bytes 415880 | tf_op jit(solution)/shard_map/ppermute | solution.py:299
  112.5 0.7 copy-start.3
  112.5 0.7 copy-start.4
  112.6 0.7 copy-start.5
  112.6 0.8 copy-start.6
  115.8 21.5 %collective-permute-start.12 = (bf16[128,1444]{1,0:T(8,128)(2,1)}, bf16[128,1444]{1,0:T(8,128)(2,1)S(1)}, u32[]{:S(2)}, u32[]{:S(2)}) collective-permute-start(bf16[128,1444]{1,0:T(8,128)(2,1)} %gather.3), channel_id=1, source_target_pairs={{0,2},{1,3},{2,0},{3,1},{4,6},{5,7},{6,4},{7,5},{8,10},{9,11},{10,... | collective-permute-start | bytes 1109000 | tf_op jit(solution)/shard_map/ppermute | solution.py:284
  120.0 2.4 %collective-permute-start.13 = (bf16[1,24,1444]{2,1,0:T(8,128)(2,1)}, bf16[1,24,1444]{2,1,0:T(8,128)(2,1)S(1)}, u32[]{:S(2)}, u32[]{:S(2)}) collective-permute-start(bf16[1,24,1444]{2,1,0:T(8,128)(2,1)} %get-tuple-element.197), channel_id=1, source_target_pairs={{0,4},{4,0},{8,12},{12,8},{16,20},{20,16},{24,28},{28,24},{1,5},{5... | collective-permute-start | bytes 207944 | tf_op jit(solution)/shard_map/ppermute | solution.py:299
  120.0 3.7 %collective-permute-start.14 = (bf16[1,24,1444]{2,1,0:T(8,128)(2,1)}, bf16[1,24,1444]{2,1,0:T(8,128)(2,1)S(1)}, u32[]{:S(2)}, u32[]{:S(2)}) collective-permute-start(bf16[1,24,1444]{2,1,0:T(8,128)(2,1)} %get-tuple-element.198), channel_id=1, source_target_pairs={{0,8},{4,12},{8,0},{12,4},{16,24},{20,28},{24,16},{28,20},{1,9},{5... | collective-permute-start | bytes 207944 | tf_op jit(solution)/shard_map/ppermute | solution.py:299
  120.3 6.0 %collective-permute-start.15 = (bf16[1,24,1444]{2,1,0:T(8,128)(2,1)}, bf16[1,24,1444]{2,1,0:T(8,128)(2,1)S(1)}, u32[]{:S(2)}, u32[]{:S(2)}) collective-permute-start(bf16[1,24,1444]{2,1,0:T(8,128)(2,1)} %get-tuple-element.199), channel_id=1, source_target_pairs={{0,12},{4,8},{8,4},{12,0},{16,28},{20,24},{24,20},{28,16},{1,13},{... | collective-permute-start | bytes 207944 | tf_op jit(solution)/shard_map/ppermute | solution.py:299
  122.1 8.7 %collective-permute-start.16 = (bf16[1,24,1444]{2,1,0:T(8,128)(2,1)}, bf16[1,24,1444]{2,1,0:T(8,128)(2,1)S(1)}, u32[]{:S(2)}, u32[]{:S(2)}) collective-permute-start(bf16[1,24,1444]{2,1,0:T(8,128)(2,1)} %get-tuple-element.200), channel_id=1, source_target_pairs={{0,16},{4,20},{8,24},{12,28},{16,0},{20,4},{24,8},{28,12},{1,17},{... | collective-permute-start | bytes 207944 | tf_op jit(solution)/shard_map/ppermute | solution.py:299
  122.4 9.6 %copy-start.8 = (bf16[1,24,1444]{2,1,0:T(8,128)(2,1)}, bf16[1,24,1444]{2,1,0:T(8,128)(2,1)S(1)}, u32[]{:S(2)}) copy-start(bf16[1,24,1444]{2,1,0:T(8,128)(2,1)S(1)} %collective-permute-done.13.refs_1_) | copy-start | bytes 207940
  122.4 8.5 %collective-permute-start.17 = (bf16[1,24,1444]{2,1,0:T(8,128)(2,1)}, bf16[1,24,1444]{2,1,0:T(8,128)(2,1)S(1)}, u32[]{:S(2)}, u32[]{:S(2)}) collective-permute-start(bf16[1,24,1444]{2,1,0:T(8,128)(2,1)} %get-tuple-element.201), channel_id=1, source_target_pairs={{0,20},{4,16},{8,28},{12,24},{16,4},{20,0},{24,12},{28,8},{1,21},{... | collective-permute-start | bytes 207944 | tf_op jit(solution)/shard_map/ppermute | solution.py:299
  123.7 8.3 %copy-start.9 = (bf16[1,24,1444]{2,1,0:T(8,128)(2,1)}, bf16[1,24,1444]{2,1,0:T(8,128)(2,1)S(1)}, u32[]{:S(2)}) copy-start(bf16[1,24,1444]{2,1,0:T(8,128)(2,1)S(1)} %collective-permute-done.14.refs_2_) | copy-start | bytes 207940
  123.7 7.2 %collective-permute-start.18 = (bf16[1,24,1444]{2,1,0:T(8,128)(2,1)}, bf16[1,24,1444]{2,1,0:T(8,128)(2,1)S(1)}, u32[]{:S(2)}, u32[]{:S(2)}) collective-permute-start(bf16[1,24,1444]{2,1,0:T(8,128)(2,1)} %get-tuple-element.202), channel_id=1, source_target_pairs={{0,24},{4,28},{8,16},{12,20},{16,8},{20,12},{24,0},{28,4},{1,25},{... | collective-permute-start | bytes 207944 | tf_op jit(solution)/shard_map/ppermute | solution.py:299
  126.2 5.8 %copy-start.10 = (bf16[1,24,1444]{2,1,0:T(8,128)(2,1)}, bf16[1,24,1444]{2,1,0:T(8,128)(2,1)S(1)}, u32[]{:S(2)}) copy-start(bf16[1,24,1444]{2,1,0:T(8,128)(2,1)S(1)} %collective-permute-done.15.refs_3_) | copy-start | bytes 207940
  126.2 5.8 %collective-permute-start.19 = (bf16[1,24,1444]{2,1,0:T(8,128)(2,1)}, bf16[1,24,1444]{2,1,0:T(8,128)(2,1)S(1)}, u32[]{:S(2)}, u32[]{:S(2)}) collective-permute-start(bf16[1,24,1444]{2,1,0:T(8,128)(2,1)} %get-tuple-element.203), channel_id=1, source_target_pairs={{0,28},{4,24},{8,20},{12,16},{16,12},{20,8},{24,4},{28,0},{1,29},{... | collective-permute-start | bytes 207944 | tf_op jit(solution)/shard_map/ppermute | solution.py:299
  130.8 1.2 copy-start.11
  130.8 27.2 %collective-permute-start.20 = (bf16[128,1444]{1,0:T(8,128)(2,1)}, bf16[128,1444]{1,0:T(8,128)(2,1)}, u32[]{:S(2)}, u32[]{:S(2)}) collective-permute-start(bf16[128,1444]{1,0:T(8,128)(2,1)} %gather.4), channel_id=1, source_target_pairs={{0,1},{1,0},{2,3},{3,2},{4,5},{5,4},{6,7},{7,6},{8,9},{9,8},{10,11... | collective-permute-start | bytes 1109000 | tf_op jit(solution)/shard_map/ppermute | solution.py:284
  130.9 1.1 copy-start.12
  130.9 1.1 copy-start.13
  132.0 0.6 copy-start.14
  135.1 22.9 %collective-permute-start.21 = (bf16[128,1444]{1,0:T(8,128)(2,1)}, bf16[128,1444]{1,0:T(8,128)(2,1)}, u32[]{:S(2)}, u32[]{:S(2)}) collective-permute-start(bf16[128,1444]{1,0:T(8,128)(2,1)} %gather.5), channel_id=1, source_target_pairs={{0,3},{1,2},{2,1},{3,0},{4,7},{5,6},{6,5},{7,4},{8,11},{9,10},{10,... | collective-permute-start | bytes 1109000 | tf_op jit(solution)/shard_map/ppermute | solution.py:284
  137.3 20.7 %copy-start.7 = (bf16[128,1444]{1,0:T(8,128)(2,1)}, bf16[128,1444]{1,0:T(8,128)(2,1)S(1)}, u32[]{:S(2)}) copy-start(bf16[128,1444]{1,0:T(8,128)(2,1)S(1)} %collective-permute-done.12.refs_1_) | copy-start | bytes 1108996
  137.3 20.8 %all-to-all-start.4 = ((bf16[8,1,24,1444]{3,2,1,0:T(8,128)(2,1)}), bf16[8,1,24,1444]{3,2,1,0:T(8,128)(2,1)S(1)}, u32[]{:S(2)}, u32[]{:S(2)}) async-start(bf16[8,1,24,1444]{3,2,1,0:T(8,128)(2,1)} %get-tuple-element.217), calls=%async_computation.4 | async-start | bytes 1179648 | tf_op jit(solution)/shard_map/all_to_all | solution.py:287
  158.1 0.8 copy-start
